TPU v7x, 256 devices: a whole 4x4x8 slice. The times are simulated.
256 devices in a mesh: head: 8 (over y, z_lo), tensor: 32 (over z_hi, x, core).
Axes of the slice: x: 4, y: 4, z: 8 (z_hi: 4, z_lo: 2; z = z_hi * 2 + z_lo), core: 2. Of those that a mesh axis runs over, the one named last changes fastest.
Arguments:
- tokens: bfloat16 [2048, 8192], P('head', 'tensor'), may hold values from -21 to 21
- w_query: bfloat16 [8192, 8192], P(None, 'tensor'), may hold values from -0.25 to 0.25
- w_key: bfloat16 [8192, 1024], P('tensor'), may hold values from -0.0625 to 0.0625
- w_value: bfloat16 [8192, 1024], P('tensor'), may hold values from -0.0625 to 0.0625
- w_out: bfloat16 [8192, 8192], P('tensor'), may hold values from -0.0625 to 0.0625
- down_query: bfloat16 [8, 8192, 64], P('head', 'tensor'), may hold values from -0.0625 to 0.0625
- up_query: bfloat16 [8, 64, 8192], P('head', None, 'tensor'), may hold values from -0.75 to 0.75
- down_key: bfloat16 [8, 8192, 64], P('head', 'tensor'), may hold values from -0.0625 to 0.0625
- up_key: bfloat16 [8, 64, 1024], P('head'), may hold values from -0.75 to 0.75
- down_value: bfloat16 [8, 8192, 64], P('head', 'tensor'), may hold values from -0.0625 to 0.0625
- up_value: bfloat16 [8, 64, 1024], P('head'), may hold values from -0.75 to 0.75
- down_out: bfloat16 [8, 8192, 64], P('head', 'tensor'), may hold values from -0.0625 to 0.0625
- up_out: bfloat16 [8, 64, 8192], P('head', None, 'tensor'), may hold values from -0.75 to 0.75
Outputs:
- layer_out: bfloat16 [2048, 8192], P('head', 'tensor')
All inputs are finite; a program needn't handle non-finite values.
Results may differ from a plain program's by a relative error of at most 0.03.
Values may be sent and summed in bfloat16 or wider, within the bound.
No kernel may reach another device: no remote copies, remote signals or barrier semaphores. Data moves between devices by JAX's collectives and lax.ppermute only.
A program may use at most 128 MiB of HBM per device.

v0:
```python
import functools
import math

import jax
import jax.numpy as jnp
from jax import lax
from jax.experimental import pallas as pl
from jax.experimental.pallas import tpu as pltpu
from jax.sharding import PartitionSpec as P

HEAD_DIM = 128
ADAPTER_SCALE = 2.0
NZ, NX, NC = 4, 4, 2
NH = 8
RANK = 64
SCALE = ADAPTER_SCALE / NH
BF = jnp.bfloat16
F32 = jnp.float32
VMEM = pl.BlockSpec(memory_space=pltpu.VMEM)
HBM = pl.BlockSpec(memory_space=pltpu.HBM)
TINY = pl.CostEstimate(flops=1000, bytes_accessed=1000, transcendentals=0)
SMEM = pl.BlockSpec(memory_space=pltpu.SMEM)


def tensor_perm(dz, dx, dc):
    pairs = []
    for t in range(NZ * NX * NC):
        z, x, c = t // (NX * NC), (t // NC) % NX, t % NC
        to = (((z - dz) % NZ) * NX + (x - dx) % NX) * NC + (c ^ dc)
        pairs.append((t, to))
    return pairs


def from_core(a):
    return lax.ppermute(a, "tensor", tensor_perm(0, 0, 1))


def from_x(a, d):
    return lax.ppermute(a, "tensor", tensor_perm(0, d, 0))


def from_z(a, d):
    return lax.ppermute(a, "tensor", tensor_perm(d, 0, 0))


def from_head(a, d):
    return lax.ppermute(a, "head", [(h, (h - d) % NH) for h in range(NH)])


def swap_all(a, axis, groups=None):
    return lax.all_to_all(a, axis, 0, 0, axis_index_groups=groups, tiled=True)


def tensor_groups(key):
    groups = {}
    for t in range(NZ * NX * NC):
        groups.setdefault(key(t // (NX * NC), (t // NC) % NX, t % NC), []).append(t)
    return list(groups.values())


def swap_x(a):
    return swap_all(a, "tensor", tensor_groups(lambda z, x, c: (z, c)))


def swap_z(a):
    return swap_all(a, "tensor", tensor_groups(lambda z, x, c: (x, c)))


def swap_xz(a):
    return swap_all(a, "tensor", tensor_groups(lambda z, x, c: c))


def dot(a, b):
    return jnp.dot(a, b, preferred_element_type=F32)


def dot_t(a, b):
    return lax.dot_general(a, b, (((1,), (1,)), ((), ())), preferred_element_type=F32)


def join(parts):
    width = sum(a.shape[-1] for a in parts)
    total, start = None, 0
    for a in parts:
        edges = [(0, 0, 0)] * (a.ndim - 1) + [(start, width - start - a.shape[-1], 0)]
        piece = lax.pad(a, jnp.zeros((), a.dtype), edges)
        total = piece if total is None else total + piece
        start += a.shape[-1]
    return total


def tie(*parts):
    return lax.optimization_barrier(parts)


def at(start, size, unit=128):
    return pl.ds(pl.multiple_of(start, unit), size)


def struct(shape, dtype):
    return jax.ShapeDtypeStruct(shape, dtype)


def fetching(kernel, held, *refs):
    refs, extra = list(refs[:-len(held) - 1]), refs[-len(held) - 1 :]
    buffers, sem = extra[:-1], extra[-1]
    copies = [
        pltpu.make_async_copy(refs[place], buffer, sem.at[i])
        for i, (place, buffer) in enumerate(zip(held, buffers))
    ]
    for copy in copies:
        copy.start()
    for copy in copies:
        copy.wait()
    for place, buffer in zip(held, buffers):
        refs[place] = buffer
    kernel(*refs)


def call(kernel, out_shape, args, scratch=(), held=(), mib=24):
    specs = [SMEM] + [HBM if i in held else VMEM for i in range(1, len(args))]
    scratch = list(scratch)
    if held:
        kernel = functools.partial(fetching, kernel, tuple(held))
        scratch += [pltpu.VMEM(args[i].shape, args[i].dtype) for i in held]
        scratch += [pltpu.SemaphoreType.DMA((len(held),))]
    return pl.pallas_call(
        kernel,
        out_shape=out_shape,
        in_specs=specs,
        out_specs=jax.tree.map(lambda _: VMEM, out_shape),
        scratch_shapes=scratch,
        compiler_params=pltpu.CompilerParams(vmem_limit_bytes=mib * 2**20),
        cost_estimate=TINY,
    )(*args)


PARTS = 7


def factor(packs, i):
    feats = packs.shape[2] // PARTS
    return packs[:, :, i * feats : (i + 1) * feats].reshape(NH * RANK, feats)


def kv_kernel(pos, tokens, tok_sib, wk, wv, wk_sib, wv_sib, own, s1, s2, s3, both):
    x, c = pos[1], pos[3]
    half, width = tok_sib.shape[0], wk.shape[1]
    mine = tokens[at(c * half, half), :]
    for i, (w, w_sib) in enumerate(((wk, wk_sib), (wv, wv_sib))):
        part = dot(mine, w[...]) + dot(tok_sib[...], w_sib[...])
        for g in range(width // HEAD_DIM):
            base = ((g % 2) * NZ * 2 + (g // 2) * 2 + i) * HEAD_DIM
            both[:, base : base + HEAD_DIM] = part[:, g * HEAD_DIM : (g + 1) * HEAD_DIM]
    for d, out in enumerate((own, s1, s2, s3)):
        xh = lax.rem(x + NX - d, NX) // 2
        out[...] = both[:, at(xh * width, width)].astype(out.dtype)


def kv_middle_kernel(pos, a0, a1, a2, a3, own, s1, s2, s3):
    z = pos[2]
    width = own.shape[1]
    for d, out in enumerate((own, s1, s2, s3)):
        cols = at(lax.rem(z + NZ - d, NZ) * width, width)
        total = a0[:, cols] + a1[:, cols].astype(F32)
        total = total + a2[:, cols].astype(F32) + a3[:, cols].astype(F32)
        out[...] = total.astype(out.dtype)


def rank_kernel(pos, tokens, packs, mine, send, stack):
    c = pos[3]
    half = mine.shape[0]
    feats = tokens.shape[1]
    for d in range(NH):
        for p in range(3):
            row = (p * NH + d) * RANK
            stack[row : row + RANK, :] = packs[d, :, p * feats : (p + 1) * feats]
    mine[...] = dot_t(tokens[at(c * half, half), :], stack[...])
    send[...] = dot_t(tokens[at((1 - c) * half, half), :], stack[...]).astype(BF)


def rank_split_kernel(pos, mine, recv, out):
    out[...] = (mine[...] + recv[...].astype(F32)).reshape(out.shape).astype(BF)


def rank_sum_kernel(pos, parts, out):
    total = parts[0].astype(F32)
    for i in range(1, NZ * NX):
        total = total + parts[i].astype(F32)
    for i in range(NZ * NX):
        out[i] = total.astype(BF)


def gather_ranks(pieces, cols):
    chips, rows, _ = pieces.shape
    part = pieces[:, :, cols].astype(F32)
    return part.reshape(chips * rows, part.shape[2]).astype(BF)


def kv_final_kernel(pos, pieces, a0, a1, a2, a3, early, out):
    n = NH * RANK
    up = factor(early, 4)
    kv = a0[...] + a1[...].astype(F32) + a2[...].astype(F32) + a3[...].astype(F32)
    low_k = dot(gather_ranks(pieces, slice(n, 2 * n)), up[:, :HEAD_DIM])
    low_v = dot(gather_ranks(pieces, slice(2 * n, 3 * n)), up[:, HEAD_DIM:])
    out[:, :HEAD_DIM] = (kv[:, :HEAD_DIM] + low_k * SCALE).astype(BF)
    out[:, HEAD_DIM:] = (kv[:, HEAD_DIM:] + low_v * SCALE).astype(BF)


def attend_kernel(
    pos, pieces, q_mine, q_recv, early, early_sib, kv_mine, kv_recv, out, kv, q
):
    c = pos[3]
    rank = gather_ranks(pieces, slice(0, NH * RANK))
    feats = early.shape[2] // PARTS
    half = q.shape[0]
    low = dot(rank, factor(early, 3)) * SCALE
    low_sib = dot(rank, factor(early_sib, 3)) * SCALE
    q[:, :feats] = (q_mine[...] + low).astype(BF)
    q[:, feats:] = (q_recv[...] + low_sib).astype(BF)
    kv[at(c * half, half), :] = kv_mine[...]
    kv[at((1 - c) * half, half), :] = kv_recv[...]
    k, v = kv[:, :HEAD_DIM], kv[:, HEAD_DIM:]
    rows = lax.broadcasted_iota(jnp.int32, (half, 2 * half), 0) + c * half
    causal = rows >= lax.broadcasted_iota(jnp.int32, (half, 2 * half), 1)
    for head in range(2 * feats // HEAD_DIM):
        cols = slice(head * HEAD_DIM, (head + 1) * HEAD_DIM)
        scores = dot_t(q[:, cols], k) * (1.0 / math.sqrt(HEAD_DIM))
        scores = jnp.where(causal, scores, -jnp.inf)
        weights = jnp.exp(scores - jnp.max(scores, axis=-1, keepdims=True))
        probs = (weights / jnp.sum(weights, axis=-1, keepdims=True)).astype(BF)
        out[:, cols] = dot(probs, v).astype(BF)


def query_kernel(pos, tok, w, mine, send, total):
    c = pos[3]
    step = pl.program_id(0)

    @pl.when(step == 0)
    def _():
        total[...] = jnp.zeros_like(total)

    part = dot(tok[0], w[0])
    for i in range(1, tok.shape[0]):
        part = part + dot(tok[i], w[i])
    total[...] += part

    @pl.when(step == pl.num_programs(0) - 1)
    def _():
        half = mine.shape[0]
        mine[...] = total[at(c * half, half), :]
        send[...] = total[at((1 - c) * half, half), :]


def query(pos, toks, w_query):
    blocks, rows, feats = toks.shape
    half = rows // NC
    steps = 4
    part = pl.BlockSpec((blocks // steps, rows, feats), lambda d, pos: (d, 0, 0))
    return pl.pallas_call(
        query_kernel,
        grid_spec=pltpu.PrefetchScalarGridSpec(
            num_scalar_prefetch=1,
            grid=(steps,),
            in_specs=[part, part],
            out_specs=[pl.BlockSpec((half, feats), lambda d, pos: (0, 0))] * 2,
            scratch_shapes=[pltpu.VMEM((rows, feats), F32)],
        ),
        out_shape=[struct((half, feats), F32)] * 2,
        compiler_params=pltpu.CompilerParams(vmem_limit_bytes=40 * 2**20),
        cost_estimate=TINY,
    )(pos, toks, w_query)


SPLIT = 4


def out_kernel(pos, att, w, w_sib, out, here, here_sib, sem):
    z = pos[2]
    blocks = NX * NZ
    width = att.shape[1]
    feats = width // NC
    part_rows = feats // SPLIT

    def fetch(k):
        cols = slice(k * width, (k + 1) * width)
        copies = []
        for j in range(SPLIT):
            rows = slice(j * part_rows, (j + 1) * part_rows)
            copies.append(pltpu.make_async_copy(w.at[rows, cols], here.at[k, rows], sem.at[2 * k]))
            copies.append(
                pltpu.make_async_copy(
                    w_sib.at[rows, cols], here_sib.at[k, rows], sem.at[2 * k + 1]
                )
            )
        return copies

    for k in range(blocks):
        for copy in fetch(k):
            copy.start()

    def step(k, carry):
        some = pl.ds(0, width)
        pltpu.make_async_copy(w.at[:, some], here.at[k], sem.at[2 * k]).wait()
        pltpu.make_async_copy(w_sib.at[:, some], here_sib.at[k], sem.at[2 * k + 1]).wait()
        part = dot(att[:, :feats], here[k]) + dot(att[:, feats:], here_sib[k])
        out[k % NX, lax.rem(k // NX + NZ - z, NZ)] = part.astype(out.dtype)
        return carry

    lax.fori_loop(0, blocks, step, 0)


def out_partial(pos, att, w_out, w_sib):
    half, width = att.shape
    feats = width // NC
    blocks = NX * NZ
    return pl.pallas_call(
        out_kernel,
        in_specs=[SMEM, VMEM, HBM, HBM],
        out_specs=VMEM,
        out_shape=struct((NX, NZ, half, width), BF),
        scratch_shapes=[pltpu.VMEM((blocks, feats, width), BF)] * 2
        + [pltpu.SemaphoreType.DMA((2 * blocks,))],
        compiler_params=pltpu.CompilerParams(vmem_limit_bytes=40 * 2**20),
        cost_estimate=TINY,
    )(pos, att, w_out, w_sib)


def out_rank_kernel(pos, att, early, early_sib, out):
    feats = early.shape[2] // PARTS
    rank = dot_t(att[:, :feats], factor(early, 5))
    rank = rank + dot_t(att[:, feats:], factor(early_sib, 5))
    for j in range(NZ):
        out[j] = rank.astype(BF)


def out_rank_sum_kernel(pos, a, out):
    total = a[0].astype(F32) + a[1].astype(F32) + a[2].astype(F32) + a[3].astype(F32)
    for j in range(NX):
        out[j] = total.astype(BF)


def final_kernel(pos, a0, a1, a2, a3, r, early, early_sib, mine, send):
    c = pos[3]
    feats = mine.shape[1]
    rank = r[0].astype(F32) + r[1].astype(F32) + r[2].astype(F32) + r[3].astype(F32)
    rank = rank.astype(BF)

    def total(cols):
        part = a0[:, cols].astype(F32) + a1[:, cols].astype(F32)
        return part + a2[:, cols].astype(F32) + a3[:, cols].astype(F32)

    low = dot(rank, factor(early, 6)) * SCALE
    low_sib = dot(rank, factor(early_sib, 6)) * SCALE
    mine[...] = (total(at(c * feats, feats)) + low).astype(BF)
    send[...] = (total(at((1 - c) * feats, feats)) + low_sib).astype(BF)


def join_kernel(pos, mine, recv, out):
    c = pos[3]
    half = mine.shape[0]
    out[at(c * half, half), :] = mine[...]
    out[at((1 - c) * half, half), :] = recv[...]


def body(
    tokens,
    w_query,
    w_key,
    w_value,
    w_out,
    down_query,
    up_query,
    down_key,
    up_key,
    down_value,
    up_value,
    down_out,
    up_out,
):
    h = lax.axis_index("head")
    t = lax.axis_index("tensor")
    c = t % NC
    x = (t // NC) % NX
    z = t // (NX * NC)
    pos = jnp.stack([h, x, z, c]).astype(jnp.int32)
    rows, feats = tokens.shape
    half = rows // NC
    n = NH * RANK
    vm = pltpu.VMEM
    x_groups = tensor_groups(lambda z, x, c: (z, c))

    def four(shape):
        return [struct(shape, F32)] + [struct(shape, BF)] * 3

    tok_zs = [tokens] + [from_z(tokens, d) for d in (1, 2, 3)]
    g = t // 4
    downs = [jnp.swapaxes(a, 1, 2) for a in (down_query, down_key, down_value, down_out)]
    up_kv = [lax.dynamic_slice_in_dim(a, g * HEAD_DIM, HEAD_DIM, 2) for a in (up_key, up_value)]
    early = join([*downs[:3], up_query, *up_kv, downs[3], up_out])
    early = swap_all(jnp.broadcast_to(early, (NH, *early.shape[1:])), "head")

    tok_all = lax.all_gather(tokens[None], "tensor", axis=0, tiled=True)

    tok_sib = from_core(lax.dynamic_slice_in_dim(tokens, (1 - c) * half, half, 0))
    own, *sends = call(
        kv_kernel,
        four((half, NZ * 2 * HEAD_DIM)),
        (pos, tokens, tok_sib, w_key, w_value, from_core(w_key), from_core(w_value)),
        [vm((half, 2 * w_key.shape[1]), F32)],
        held=(1, 3, 4),
    )
    kv_x = [own] + [from_x(s, d) for d, s in zip((1, 2, 3), sends)]
    early, kv_x = tie(early, kv_x)

    mine, send = call(
        rank_kernel,
        [struct((half, 3 * n), F32), struct((half, 3 * n), BF)],
        (pos, tokens, early),
        [vm((3 * n, feats), BF)],
        held=(1,),
    )
    chips = NZ * NX
    pieces = call(
        rank_split_kernel,
        struct((chips, half // chips, 3 * n), BF),
        (pos, mine, from_core(send)),
    )
    early_sib = from_core(early)
    own, *sends = call(kv_middle_kernel, four((half, 2 * HEAD_DIM)), (pos, *kv_x))
    kv_z = [own] + [from_z(s, d) for d, s in zip((1, 2, 3), sends)]
    pieces = swap_xz(pieces)
    pieces, early_sib, w_out_now, kv_z = tie(pieces, early_sib, w_out, kv_z)
    w_o_sib = from_core(w_out_now)
    pieces = call(rank_sum_kernel, struct(pieces.shape, BF), (pos, pieces))
    pieces = swap_xz(pieces)

    q_mine, q_send = query(pos, tok_all, w_query.reshape(NZ * NX * NC, feats, feats))
    q_recv = from_core(q_send)
    pieces, w_o_sib, q_recv = tie(pieces, w_o_sib, q_recv)
    kv_mine = call(kv_final_kernel, struct((half, 2 * HEAD_DIM), BF), (pos, pieces, *kv_z, early))

    att = call(
        attend_kernel,
        struct((half, NC * feats), BF),
        (pos, pieces, q_mine, q_recv, early, early_sib, kv_mine, from_core(kv_mine)),
        [vm((rows, 2 * HEAD_DIM), BF), vm((half, NC * feats), BF)],
    )

    rank_o = call(out_rank_kernel, struct((NZ, half, n), BF), (pos, att, early, early_sib))
    att, rank_o = tie(att, rank_o)
    out = out_partial(pos, att, w_out, w_o_sib)
    out_x = lax.psum_scatter(
        out, "tensor", scatter_dimension=0, tiled=True, axis_index_groups=x_groups
    )
    rank_o, _ = tie(rank_o, out)
    rank_o = call(out_rank_sum_kernel, struct((NX, half, n), BF), (pos, swap_z(rank_o)))
    rank_o = swap_x(rank_o)
    out_x = [out_x[0, i] for i in range(NZ)]
    out_z = [out_x[0]] + [from_z(out_x[NZ - d], d) for d in (1, 2, 3)]
    mine, send = call(
        final_kernel, [struct((half, feats), BF)] * 2, (pos, *out_z, rank_o, early, early_sib)
    )
    return call(join_kernel, struct((rows, feats), BF), (pos, mine, from_core(send)))


def solution(mesh):
    placed = (
        P("head", "tensor"),
        P(None, "tensor"),
        P("tensor", None),
        P("tensor", None),
        P("tensor", None),
        P("head", "tensor", None),
        P("head", None, "tensor"),
        P("head", "tensor", None),
        P("head", None, None),
        P("head", "tensor", None),
        P("head", None, None),
        P("head", "tensor", None),
        P("head", None, "tensor"),
    )
    return jax.shard_map(
        body, mesh=mesh, in_specs=placed, out_specs=P("head", "tensor"), check_vma=False
    )
```

profile of v0, /device:TPU:25, one launch (start us, length us, event | category | flops | bytes accessed | tf_op | source)
XLA Modules:
  0.0 187.7 jit_solution(9913247337138523155)
XLA Ops:
  9.7 5.5 %all-to-all-start = ((bf16[8,64,1792]{2,1,0:T(8,128)(2,1)}), bf16[8,64,1792]{2,1,0:T(8,128)(2,1)S(1)}, u32[]{:S(2)}, u32[]{:S(2)}) async-start(bf16[8,64,1792]{2,1,0:T(8,128)(2,1)} %broadcast_in_dim.11), calls=%async_computation | async-start | bytes 3670016 | tf_op jit(solution)/shard_map/all_to_all | solution.py:51
  22.6 2.5 %collective-permute-start.3 = (bf16[128,1024]{1,0:T(8,128)(2,1)S(1)}, bf16[128,1024]{1,0:T(8,128)(2,1)S(1)}, u32[]{:S(2)}, u32[]{:S(2)}) collective-permute-start(bf16[128,1024]{1,0:T(8,128)(2,1)S(1)} %get-tuple-element.38), channel_id=1, source_target_pairs={{0,6},{1,7},{2,0},{3,1},{4,2},{5,3},{6,4},{7,5},{8,14},{9,15},{10,... | collective-permute-start | bytes 786440 | tf_op jit(solution)/shard_map/ppermute | solution.py:39
  26.2 9.7 %collective-permute-done.3.a1 = bf16[128,1024]{1,0:T(8,128)(2,1)S(1)} collective-permute-done((bf16[128,1024]{1,0:T(8,128)(2,1)S(1)}, bf16[128,1024]{1,0:T(8,128)(2,1)S(1)}, u32[]{:S(2)}, u32[]{:S(2)}) %collective-permute-start.3) | collective-permute-done | bytes 262176 | tf_op jit(solution)/shard_map/ppermute | solution.py:39
  35.9 5.4 %collective-permute-done.5.a3 = bf16[128,1024]{1,0:T(8,128)(2,1)S(1)} collective-permute-done((bf16[128,1024]{1,0:T(8,128)(2,1)S(1)}, bf16[128,1024]{1,0:T(8,128)(2,1)S(1)}, u32[]{:S(2)}, u32[]{:S(2)}) %collective-permute-start.5) | collective-permute-done | bytes 262176 | tf_op jit(solution)/shard_map/ppermute | solution.py:39
  44.0 2.5 %collective-permute-done.6.recv = bf16[128,1536]{1,0:T(8,128)(2,1)S(1)} collective-permute-done((bf16[128,1536]{1,0:T(8,128)(2,1)S(1)}, bf16[128,1536]{1,0:T(8,128)(2,1)S(1)}, u32[]{:S(2)}, u32[]{:S(2)}) %collective-permute-start.6) | collective-permute-done | bytes 393248 | tf_op jit(solution)/shard_map/ppermute | solution.py:35
  47.9 8.5 %all-to-all-start.1 = ((bf16[16,8,1536]{2,1,0:T(8,128)(2,1)}), bf16[16,8,1536]{2,1,0:T(8,128)(2,1)S(1)}, u32[]{:S(2)}, u32[]{:S(2)}) async-start(bf16[16,8,1536]{2,1,0:T(8,128)(2,1)} %shard_map.129), calls=%async_computation.1 | async-start | bytes 786432 | tf_op jit(solution)/shard_map/all_to_all | solution.py:51
  58.0 3.6 %collective-permute-start.8 = (bf16[128,256]{1,0:T(8,128)(2,1)S(1)}, bf16[128,256]{1,0:T(8,128)(2,1)S(1)}, u32[]{:S(2)}, u32[]{:S(2)}) collective-permute-start(bf16[128,256]{1,0:T(8,128)(2,1)S(1)} %get-tuple-element.49), channel_id=1, source_target_pairs={{0,24},{1,25},{2,26},{3,27},{4,28},{5,29},{6,30},{7,31},{8,0},{9,1... | collective-permute-start | bytes 196616 | tf_op jit(solution)/shard_map/ppermute | solution.py:43
  65.7 12.4 %collective-permute-done.8.a1 = bf16[128,256]{1,0:T(8,128)(2,1)S(1)} collective-permute-done((bf16[128,256]{1,0:T(8,128)(2,1)S(1)}, bf16[128,256]{1,0:T(8,128)(2,1)S(1)}, u32[]{:S(2)}, u32[]{:S(2)}) %collective-permute-start.8) | collective-permute-done | bytes 65568 | tf_op jit(solution)/shard_map/ppermute | solution.py:43
  78.2 4.0 %collective-permute-start.11 = (bf16[256,8192]{1,0:T(8,128)(2,1)}, bf16[256,8192]{1,0:T(8,128)(2,1)}, u32[]{:S(2)}, u32[]{:S(2)}) collective-permute-start(bf16[256,8192]{1,0:T(8,128)(2,1)} %w.1), channel_id=1, source_target_pairs={{0,1},{1,0},{2,3},{3,2},{4,5},{5,4},{6,7},{7,6},{8,9},{9,8},{10,11... | collective-permute-start | bytes 12582920 | tf_op jit(solution)/shard_map/ppermute | solution.py:35
  83.6 8.6 %all-to-all-start.2 = ((bf16[16,8,1536]{2,1,0:T(8,128)(2,1)}), bf16[16,8,1536]{2,1,0:T(8,128)(2,1)S(1)}, u32[]{:S(2)}, u32[]{:S(2)}) async-start(bf16[16,8,1536]{2,1,0:T(8,128)(2,1)} %shard_map.131), calls=%async_computation.2 | async-start | bytes 786432 | tf_op jit(solution)/shard_map/all_to_all | solution.py:51
  94.0 2.2 %copy-done.1 = bf16[8192,256]{1,0:T(8,128)(2,1)S(1)} copy-done((bf16[8192,256]{1,0:T(8,128)(2,1)S(1)}, bf16[8192,256]{1,0:T(8,128)(2,1)}, u32[]{:S(2)}) %copy-start.1) | copy-done | bytes 4194328
  96.2 2.2 %copy-done.3 = bf16[8192,256]{1,0:T(8,128)(2,1)S(1)} copy-done((bf16[8192,256]{1,0:T(8,128)(2,1)S(1)}, bf16[8192,256]{1,0:T(8,128)(2,1)}, u32[]{:S(2)}) %copy-start.3) | copy-done | bytes 4194328
  98.4 2.4 %shard_map.132 = (f32[128,256]{1,0:T(8,128)S(1)}, f32[128,256]{1,0:T(8,128)S(1)}) custom-call(s32[4]{0:T(128)S(1)} %pad_add_fusion.refs_0_.pos, bf16[32,256,256]{2,1,0:T(8,128)(2,1)S(1)} %bitcast.21, bf16[32,256,256]{2,1,0:T(8,128)(2,1)S(1)} %bitcast.20), custom_call_target="tpu_custom_call" | custom-call | flops 1000 | bytes 1000 | tf_op jit(solution)/shard_map/pallas_call | solution.py:260
  101.1 5.3 %all-to-all-done.2.pieces = bf16[16,8,1536]{2,1,0:T(8,128)(2,1)S(1)} async-done(((bf16[16,8,1536]{2,1,0:T(8,128)(2,1)}), bf16[16,8,1536]{2,1,0:T(8,128)(2,1)S(1)}, u32[]{:S(2)}, u32[]{:S(2)}) %all-to-all-start.2) | async-done | bytes 393248 | tf_op jit(solution)/shard_map/all_to_all | solution.py:51
  110.1 2.5 %shard_map.134.att = bf16[128,512]{1,0:T(8,128)(2,1)S(1)} custom-call(s32[4]{0:T(128)S(1)} %pad_add_fusion.refs_0_.pos, bf16[16,8,1536]{2,1,0:T(8,128)(2,1)S(1)} %all-to-all-done.2.pieces, f32[128,256]{1,0:T(8,128)S(1)} %get-tuple-element.56.q_mine, f32[128,256]{1,0:T(8,128)S(1)} %collective-permute-done.12.q_recv, ...), custom_call_target="tpu_custom_call" | custom-call | flops 1000 | bytes 1000 | tf_op jit(solution)/shard_map/pallas_call | solution.py:127
  114.4 5.6 %shard_map.136 = bf16[4,4,128,512]{3,2,1,0:T(8,128)(2,1)S(1)} custom-call(s32[4]{0:T(128)S(1)} %pad_add_fusion.refs_0_.pos, bf16[128,512]{1,0:T(8,128)(2,1)S(1)} %shard_map.134.att, bf16[256,8192]{1,0:T(8,128)(2,1)S(1)} %copy-done.2, bf16[256,8192]{1,0:T(8,128)(2,1)} %collective-permute-done.11.w_sib), custom_call_target="tpu_custom_call" | custom-call | flops 1000 | bytes 1000 | tf_op jit(solution)/shard_map/pallas_call | solution.py:317
  121.4 17.2 %all_to_all.25.a = bf16[4,128,512]{2,1,0:T(8,128)(2,1)S(1)} all-to-all(bf16[4,128,512]{2,1,0:T(8,128)(2,1)S(1)} %shard_map.135), channel_id=1, replica_groups={{0,8,16,24},{1,9,17,25},{2,10,18,26},{3,11,19,27},{4,12,20,28},{5,13,21..., dimensions={0} | all-to-all | bytes 1048576 | tf_op jit(solution)/shard_map/all_to_all | solution.py:51
  140.0 3.5 %all-to-all-start.4 = ((bf16[4,128,512]{2,1,0:T(8,128)(2,1)}), bf16[4,128,512]{2,1,0:T(8,128)(2,1)S(1)}, u32[]{:S(2)}, u32[]{:S(2)}) async-start(bf16[4,128,512]{2,1,0:T(8,128)(2,1)} %shard_map.137), calls=%async_computation.5 | async-start | bytes 1048576 | tf_op jit(solution)/shard_map/all_to_all | solution.py:51
  143.5 9.7 %reduce-scatter.2.cloned.1.call-done = bf16[1,4,128,512]{3,2,1,0:T(8,128)(2,1)} async-done(((bf16[4,4,128,512]{3,2,1,0:T(8,128)(2,1)}), bf16[1,4,128,512]{3,2,1,0:T(8,128)(2,1)}) %reduce-scatter.2.cloned.1.call-update) | async-done | bytes 524304 | tf_op jit(solution)/shard_map/reduce_scatter | solution.py:453
  154.3 2.6 %collective-permute-start.16 = (bf16[128,512]{1,0:T(8,128)(2,1)S(1)}, bf16[128,512]{1,0:T(8,128)(2,1)S(1)}, u32[]{:S(2)}, u32[]{:S(2)}) collective-permute-start(bf16[128,512]{1,0:T(8,128)(2,1)S(1)} %get-tuple-element.69), channel_id=1, source_target_pairs={{0,8},{1,9},{2,10},{3,11},{4,12},{5,13},{6,14},{7,15},{8,16},{9,17... | collective-permute-start | bytes 393224 | tf_op jit(solution)/shard_map/ppermute | solution.py:43
  156.9 6.6 %collective-permute-start.15 = (bf16[128,512]{1,0:T(8,128)(2,1)S(1)}, bf16[128,512]{1,0:T(8,128)(2,1)S(1)}, u32[]{:S(2)}, u32[]{:S(2)}) collective-permute-start(bf16[128,512]{1,0:T(8,128)(2,1)S(1)} %get-tuple-element.70), channel_id=1, source_target_pairs={{0,16},{1,17},{2,18},{3,19},{4,20},{5,21},{6,22},{7,23},{8,24},{9,... | collective-permute-start | bytes 393224 | tf_op jit(solution)/shard_map/ppermute | solution.py:43
  163.4 3.5 %collective-permute-start.14 = (bf16[128,512]{1,0:T(8,128)(2,1)S(1)}, bf16[128,512]{1,0:T(8,128)(2,1)S(1)}, u32[]{:S(2)}, u32[]{:S(2)}) collective-permute-start(bf16[128,512]{1,0:T(8,128)(2,1)S(1)} %get-tuple-element.71), channel_id=1, source_target_pairs={{0,24},{1,25},{2,26},{3,27},{4,28},{5,29},{6,30},{7,31},{8,0},{9,1... | collective-permute-start | bytes 393224 | tf_op jit(solution)/shard_map/ppermute | solution.py:43
  166.9 4.0 %collective-permute-done.15.a2 = bf16[128,512]{1,0:T(8,128)(2,1)S(1)} collective-permute-done((bf16[128,512]{1,0:T(8,128)(2,1)S(1)}, bf16[128,512]{1,0:T(8,128)(2,1)S(1)}, u32[]{:S(2)}, u32[]{:S(2)}) %collective-permute-start.15) | collective-permute-done | bytes 131104 | tf_op jit(solution)/shard_map/ppermute | solution.py:43
  170.9 5.5 %collective-permute-done.14.a1 = bf16[128,512]{1,0:T(8,128)(2,1)S(1)} collective-permute-done((bf16[128,512]{1,0:T(8,128)(2,1)S(1)}, bf16[128,512]{1,0:T(8,128)(2,1)S(1)}, u32[]{:S(2)}, u32[]{:S(2)}) %collective-permute-start.14) | collective-permute-done | bytes 131104 | tf_op jit(solution)/shard_map/ppermute | solution.py:43
  (68 shorter events, 38.8 us)
Async XLA Ops:
  9.7 32.4 %all-to-all-start = ((bf16[8,64,1792]{2,1,0:T(8,128)(2,1)}), bf16[8,64,1792]{2,1,0:T(8,128)(2,1)S(1)}, u32[]{:S(2)}, u32[]{:S(2)}) async-start(bf16[8,64,1792]{2,1,0:T(8,128)(2,1)} %broadcast_in_dim.11), calls=%async_computation | async-start | bytes 3670016 | tf_op jit(solution)/shard_map/all_to_all | solution.py:51
  15.1 78.9 %all-gather.3.cloned.1.call-start = ((), (), s32[]{:S(2)}) async-start(), calls=%async_computation.7 | async-start | bytes 4325376 | tf_op jit(solution)/shard_map/all_gather | solution.py:403
  15.9 3.0 %collective-permute-start.1 = (bf16[256,1024]{1,0:T(8,128)(2,1)S(1)}, bf16[256,1024]{1,0:T(8,128)(2,1)}, u32[]{:S(2)}, u32[]{:S(2)}) collective-permute-start(bf16[256,1024]{1,0:T(8,128)(2,1)S(1)} %copy-done.5), channel_id=1, source_target_pairs={{0,1},{1,0},{2,3},{3,2},{4,5},{5,4},{6,7},{7,6},{8,9},{9,8},{10,11... | collective-permute-start | bytes 1572872 | tf_op jit(solution)/shard_map/ppermute | solution.py:35
  17.2 2.5 %collective-permute-start.2 = (bf16[256,1024]{1,0:T(8,128)(2,1)S(1)}, bf16[256,1024]{1,0:T(8,128)(2,1)}, u32[]{:S(2)}, u32[]{:S(2)}) collective-permute-start(bf16[256,1024]{1,0:T(8,128)(2,1)S(1)} %copy-done.6), channel_id=1, source_target_pairs={{0,1},{1,0},{2,3},{3,2},{4,5},{5,4},{6,7},{7,6},{8,9},{9,8},{10,11... | collective-permute-start | bytes 1572872 | tf_op jit(solution)/shard_map/ppermute | solution.py:35
  17.3 1.6 collective-permute-start
  22.6 13.3 %collective-permute-start.3 = (bf16[128,1024]{1,0:T(8,128)(2,1)S(1)}, bf16[128,1024]{1,0:T(8,128)(2,1)S(1)}, u32[]{:S(2)}, u32[]{:S(2)}) collective-permute-start(bf16[128,1024]{1,0:T(8,128)(2,1)S(1)} %get-tuple-element.38), channel_id=1, source_target_pairs={{0,6},{1,7},{2,0},{3,1},{4,2},{5,3},{6,4},{7,5},{8,14},{9,15},{10,... | collective-permute-start | bytes 786440 | tf_op jit(solution)/shard_map/ppermute | solution.py:39
  25.1 10.8 %collective-permute-start.4 = (bf16[128,1024]{1,0:T(8,128)(2,1)S(1)}, bf16[128,1024]{1,0:T(8,128)(2,1)S(1)}, u32[]{:S(2)}, u32[]{:S(2)}) collective-permute-start(bf16[128,1024]{1,0:T(8,128)(2,1)S(1)} %get-tuple-element.39), channel_id=1, source_target_pairs={{0,4},{1,5},{2,6},{3,7},{4,0},{5,1},{6,2},{7,3},{8,12},{9,13},{10,... | collective-permute-start | bytes 786440 | tf_op jit(solution)/shard_map/ppermute | solution.py:39
  25.6 15.7 %collective-permute-start.5 = (bf16[128,1024]{1,0:T(8,128)(2,1)S(1)}, bf16[128,1024]{1,0:T(8,128)(2,1)S(1)}, u32[]{:S(2)}, u32[]{:S(2)}) collective-permute-start(bf16[128,1024]{1,0:T(8,128)(2,1)S(1)} %get-tuple-element.40), channel_id=1, source_target_pairs={{0,2},{1,3},{2,4},{3,5},{4,6},{5,7},{6,0},{7,1},{8,10},{9,11},{10,... | collective-permute-start | bytes 786440 | tf_op jit(solution)/shard_map/ppermute | solution.py:39
  42.0 36.1 %collective-permute-start.7 = (bf16[8,64,1792]{2,1,0:T(8,128)(2,1)S(1)}, bf16[8,64,1792]{2,1,0:T(8,128)(2,1)}, u32[]{:S(2)}, u32[]{:S(2)}) collective-permute-start(bf16[8,64,1792]{2,1,0:T(8,128)(2,1)S(1)} %all-to-all-done.refs_2_.early), channel_id=1, source_target_pairs={{0,1},{1,0},{2,3},{3,2},{4,5},{5,4},{6,7},{7,6},{8,9},{9,8},{10,11... | collective-permute-start | bytes 5505032 | tf_op jit(solution)/shard_map/ppermute | solution.py:35
  43.9 2.6 %collective-permute-start.6 = (bf16[128,1536]{1,0:T(8,128)(2,1)S(1)}, bf16[128,1536]{1,0:T(8,128)(2,1)S(1)}, u32[]{:S(2)}, u32[]{:S(2)}) collective-permute-start(bf16[128,1536]{1,0:T(8,128)(2,1)S(1)} %get-tuple-element.43), channel_id=1, source_target_pairs={{0,1},{1,0},{2,3},{3,2},{4,5},{5,4},{6,7},{7,6},{8,9},{9,8},{10,11... | collective-permute-start | bytes 1179656 | tf_op jit(solution)/shard_map/ppermute | solution.py:35
  47.9 30.3 %all-to-all-start.1 = ((bf16[16,8,1536]{2,1,0:T(8,128)(2,1)}), bf16[16,8,1536]{2,1,0:T(8,128)(2,1)S(1)}, u32[]{:S(2)}, u32[]{:S(2)}) async-start(bf16[16,8,1536]{2,1,0:T(8,128)(2,1)} %shard_map.129), calls=%async_computation.1 | async-start | bytes 786432 | tf_op jit(solution)/shard_map/all_to_all | solution.py:51
  58.0 20.1 %collective-permute-start.8 = (bf16[128,256]{1,0:T(8,128)(2,1)S(1)}, bf16[128,256]{1,0:T(8,128)(2,1)S(1)}, u32[]{:S(2)}, u32[]{:S(2)}) collective-permute-start(bf16[128,256]{1,0:T(8,128)(2,1)S(1)} %get-tuple-element.49), channel_id=1, source_target_pairs={{0,24},{1,25},{2,26},{3,27},{4,28},{5,29},{6,30},{7,31},{8,0},{9,1... | collective-permute-start | bytes 196616 | tf_op jit(solution)/shard_map/ppermute | solution.py:43
  61.6 16.6 %collective-permute-start.9 = (bf16[128,256]{1,0:T(8,128)(2,1)S(1)}, bf16[128,256]{1,0:T(8,128)(2,1)S(1)}, u32[]{:S(2)}, u32[]{:S(2)}) collective-permute-start(bf16[128,256]{1,0:T(8,128)(2,1)S(1)} %get-tuple-element.50), channel_id=1, source_target_pairs={{0,16},{1,17},{2,18},{3,19},{4,20},{5,21},{6,22},{7,23},{8,24},{9,... | collective-permute-start | bytes 196616 | tf_op jit(solution)/shard_map/ppermute | solution.py:43
  63.6 14.5 %collective-permute-start.10 = (bf16[128,256]{1,0:T(8,128)(2,1)S(1)}, bf16[128,256]{1,0:T(8,128)(2,1)S(1)}, u32[]{:S(2)}, u32[]{:S(2)}) collective-permute-start(bf16[128,256]{1,0:T(8,128)(2,1)S(1)} %get-tuple-element.51), channel_id=1, source_target_pairs={{0,8},{1,9},{2,10},{3,11},{4,12},{5,13},{6,14},{7,15},{8,16},{9,17... | collective-permute-start | bytes 196616 | tf_op jit(solution)/shard_map/ppermute | solution.py:43
  78.2 28.3 %collective-permute-start.11 = (bf16[256,8192]{1,0:T(8,128)(2,1)}, bf16[256,8192]{1,0:T(8,128)(2,1)}, u32[]{:S(2)}, u32[]{:S(2)}) collective-permute-start(bf16[256,8192]{1,0:T(8,128)(2,1)} %w.1), channel_id=1, source_target_pairs={{0,1},{1,0},{2,3},{3,2},{4,5},{5,4},{6,7},{7,6},{8,9},{9,8},{10,11... | collective-permute-start | bytes 12582920 | tf_op jit(solution)/shard_map/ppermute | solution.py:35
  83.6 22.9 %all-to-all-start.2 = ((bf16[16,8,1536]{2,1,0:T(8,128)(2,1)}), bf16[16,8,1536]{2,1,0:T(8,128)(2,1)S(1)}, u32[]{:S(2)}, u32[]{:S(2)}) async-start(bf16[16,8,1536]{2,1,0:T(8,128)(2,1)} %shard_map.131), calls=%async_computation.2 | async-start | bytes 786432 | tf_op jit(solution)/shard_map/all_to_all | solution.py:51
  92.2 61.0 %reduce-scatter.2.cloned.1.call-start = ((), (), s32[]{:S(2)}) async-start(), calls=%async_computation.6 | async-start | bytes 2621440 | tf_op jit(solution)/shard_map/reduce_scatter | solution.py:453
  100.8 5.7 %collective-permute-start.12 = (f32[128,256]{1,0:T(8,128)S(1)}, f32[128,256]{1,0:T(8,128)S(1)}, u32[]{:S(2)}, u32[]{:S(2)}) collective-permute-start(f32[128,256]{1,0:T(8,128)S(1)} %get-tuple-element.54), channel_id=1, source_target_pairs={{0,1},{1,0},{2,3},{3,2},{4,5},{5,4},{6,7},{7,6},{8,9},{9,8},{10,11... | collective-permute-start | bytes 393224 | tf_op jit(solution)/shard_map/ppermute | solution.py:35
  107.2 2.8 %collective-permute-start.13 = (bf16[128,256]{1,0:T(8,128)(2,1)S(1)}, bf16[128,256]{1,0:T(8,128)(2,1)S(1)}, u32[]{:S(2)}, u32[]{:S(2)}) collective-permute-start(bf16[128,256]{1,0:T(8,128)(2,1)S(1)} %shard_map.133.kv_mine), channel_id=1, source_target_pairs={{0,1},{1,0},{2,3},{3,2},{4,5},{5,4},{6,7},{7,6},{8,9},{9,8},{10,11... | collective-permute-start | bytes 196616 | tf_op jit(solution)/shard_map/ppermute | solution.py:35
  140.0 26.9 %all-to-all-start.4 = ((bf16[4,128,512]{2,1,0:T(8,128)(2,1)}), bf16[4,128,512]{2,1,0:T(8,128)(2,1)S(1)}, u32[]{:S(2)}, u32[]{:S(2)}) async-start(bf16[4,128,512]{2,1,0:T(8,128)(2,1)} %shard_map.137), calls=%async_computation.5 | async-start | bytes 1048576 | tf_op jit(solution)/shard_map/all_to_all | solution.py:51
  154.3 12.6 %collective-permute-start.16 = (bf16[128,512]{1,0:T(8,128)(2,1)S(1)}, bf16[128,512]{1,0:T(8,128)(2,1)S(1)}, u32[]{:S(2)}, u32[]{:S(2)}) collective-permute-start(bf16[128,512]{1,0:T(8,128)(2,1)S(1)} %get-tuple-element.69), channel_id=1, source_target_pairs={{0,8},{1,9},{2,10},{3,11},{4,12},{5,13},{6,14},{7,15},{8,16},{9,17... | collective-permute-start | bytes 393224 | tf_op jit(solution)/shard_map/ppermute | solution.py:43
  156.9 14.0 %collective-permute-start.15 = (bf16[128,512]{1,0:T(8,128)(2,1)S(1)}, bf16[128,512]{1,0:T(8,128)(2,1)S(1)}, u32[]{:S(2)}, u32[]{:S(2)}) collective-permute-start(bf16[128,512]{1,0:T(8,128)(2,1)S(1)} %get-tuple-element.70), channel_id=1, source_target_pairs={{0,16},{1,17},{2,18},{3,19},{4,20},{5,21},{6,22},{7,23},{8,24},{9,... | collective-permute-start | bytes 393224 | tf_op jit(solution)/shard_map/ppermute | solution.py:43
  163.4 13.0 %collective-permute-start.14 = (bf16[128,512]{1,0:T(8,128)(2,1)S(1)}, bf16[128,512]{1,0:T(8,128)(2,1)S(1)}, u32[]{:S(2)}, u32[]{:S(2)}) collective-permute-start(bf16[128,512]{1,0:T(8,128)(2,1)S(1)} %get-tuple-element.71), channel_id=1, source_target_pairs={{0,24},{1,25},{2,26},{3,27},{4,28},{5,29},{6,30},{7,31},{8,0},{9,1... | collective-permute-start | bytes 393224 | tf_op jit(solution)/shard_map/ppermute | solution.py:43
  178.2 1.5 collective-permute-start.17
  (11 other events, 77.0 us)
Sparse Core Ops, SparseCore 0:
  18.5 75.4 all-gather.2
  121.5 31.6 reduce-scatter.1
where the time goes:
time: 188 us
  waiting for transfers between devices  60.8 us (32%)
  starting transfers between devices  59.4 us (32%)
  Pallas kernels  24.2 us (13%)
  blocking collectives  17.2 us (9%)
  between operations  13.6 us (7%)
  local copies, waits for them, and re-layouts  11.6 us (6%)
    all_to_all x4, starting transfers between devices, swap_all(): return lax.all_to_all(a, axis, 0, 0, axis_index_groups=groups, tiled=True)  26 us
    ppermute x6, waiting for transfers between devices, from_z(): return lax.ppermute(a, 'tensor', tensor_perm(d, 0, 0))  21.9 us
    ppermute x6, starting transfers between devices, from_z(): return lax.ppermute(a, 'tensor', tensor_perm(d, 0, 0))  20.3 us
    all_to_all x1, blocking collectives, swap_all(): return lax.all_to_all(a, axis, 0, 0, axis_index_groups=groups, tiled=True)  17.2 us
    pallas_call x11, Pallas kernels, call(): pl.pallas_call(kernel, out_shape=out_shape, in_specs=specs, out_specs=jax...  16.3 us
    ppermute x3, waiting for transfers between devices, from_x(): return lax.ppermute(a, 'tensor', tensor_perm(0, d, 0))  15.1 us
    reduce_scatter x1, waiting for transfers between devices, body(): lax.psum_scatter(out, 'tensor', scatter_dimension=0, tiled=True, axis_ind...  9.68 us
    ppermute x9, starting transfers between devices, from_core(): return lax.ppermute(a, 'tensor', tensor_perm(0, 0, 1))  9.42 us
  transfers between devices with their start and end apart: 24, of which 13 were waited for; matrix products, arithmetic and copies ran while one was open for 1% of the time, Pallas kernels for 6%

commit v1 on v0

--- a/solution.py
+++ b/solution.py
@@ -143,6 +143,16 @@
     return packs[:, :, i * feats : (i + 1) * feats].reshape(NH * RANK, feats)
 
 
+def factors_kernel(pos, early, early_sib, up_q, up_kv, down_o, up_o):
+    feats = up_o.shape[1]
+    up_q[:, :feats] = factor(early, 3)
+    up_q[:, feats:] = factor(early_sib, 3)
+    up_kv[...] = factor(early, 4)
+    down_o[:, :feats] = factor(early, 5)
+    down_o[:, feats:] = factor(early_sib, 5)
+    up_o[...] = factor(early, 6)
+
+
 def kv_kernel(pos, tokens, tok_sib, wk, wv, wk_sib, wv_sib, own, s1, s2, s3, both):
     x, c = pos[1], pos[3]
     half, width = tok_sib.shape[0], wk.shape[1]
@@ -197,9 +207,8 @@
     return part.reshape(chips * rows, part.shape[2]).astype(BF)
 
 
-def kv_final_kernel(pos, pieces, a0, a1, a2, a3, early, out):
+def kv_final_kernel(pos, pieces, a0, a1, a2, a3, up, out):
     n = NH * RANK
-    up = factor(early, 4)
     kv = a0[...] + a1[...].astype(F32) + a2[...].astype(F32) + a3[...].astype(F32)
     low_k = dot(gather_ranks(pieces, slice(n, 2 * n)), up[:, :HEAD_DIM])
     low_v = dot(gather_ranks(pieces, slice(2 * n, 3 * n)), up[:, HEAD_DIM:])
@@ -207,17 +216,12 @@
     out[:, HEAD_DIM:] = (kv[:, HEAD_DIM:] + low_v * SCALE).astype(BF)
 
 
-def attend_kernel(
-    pos, pieces, q_mine, q_recv, early, early_sib, kv_mine, kv_recv, out, kv, q
-):
+def attend_kernel(pos, pieces, q_mine, q_recv, up_q, kv_mine, kv_recv, out, kv, q):
     c = pos[3]
-    rank = gather_ranks(pieces, slice(0, NH * RANK))
-    feats = early.shape[2] // PARTS
-    half = q.shape[0]
-    low = dot(rank, factor(early, 3)) * SCALE
-    low_sib = dot(rank, factor(early_sib, 3)) * SCALE
-    q[:, :feats] = (q_mine[...] + low).astype(BF)
-    q[:, feats:] = (q_recv[...] + low_sib).astype(BF)
+    half, feats = q_mine.shape
+    low = dot(gather_ranks(pieces, slice(0, NH * RANK)), up_q[...]) * SCALE
+    q[:, :feats] = (q_mine[...] + low[:, :feats]).astype(BF)
+    q[:, feats:] = (q_recv[...] + low[:, feats:]).astype(BF)
     kv[at(c * half, half), :] = kv_mine[...]
     kv[at((1 - c) * half, half), :] = kv_recv[...]
     k, v = kv[:, :HEAD_DIM], kv[:, HEAD_DIM:]
@@ -275,92 +279,98 @@
 SPLIT = 4
 
 
-def out_kernel(pos, att, w, w_sib, out, here, here_sib, sem):
-    z = pos[2]
-    blocks = NX * NZ
-    width = att.shape[1]
-    feats = width // NC
-    part_rows = feats // SPLIT
-
-    def fetch(k):
-        cols = slice(k * width, (k + 1) * width)
-        copies = []
-        for j in range(SPLIT):
-            rows = slice(j * part_rows, (j + 1) * part_rows)
-            copies.append(pltpu.make_async_copy(w.at[rows, cols], here.at[k, rows], sem.at[2 * k]))
-            copies.append(
+def out_kernel(pos, att, att_recv, w, w_sib, out, rows_in, here, done, sem, out_sem):
+    z, c = pos[2], pos[3]
+    rows, feats = done.shape[1:]
+    blocks = done.shape[0]
+    half = rows // NC
+    pairs = blocks // 2
+
+    for k in range(blocks):
+        cols = at((NC * k + c) * feats, feats)
+        to = slice(k % 2 * feats, (k % 2 + 1) * feats)
+        for i, a in enumerate((w, w_sib)):
+            for j in range(SPLIT):
+                part = slice(j * feats // SPLIT, (j + 1) * feats // SPLIT)
+                place = slice(i * feats + part.start, i * feats + part.stop)
                 pltpu.make_async_copy(
-                    w_sib.at[rows, cols], here_sib.at[k, rows], sem.at[2 * k + 1]
-                )
-            )
-        return copies
-
+                    a.at[part, cols], here.at[k // 2, place, to], sem.at[2 * k + i]
+                ).start()
+    rows_in[at(c * half, half), :] = att[...]
+    other = at((1 - c) * half, half)
+    rows_in[other, :feats] = att_recv[:, feats:]
+    rows_in[other, feats:] = att_recv[:, :feats]
+
+    def leave(k):
+        place = out.at[k % NX, lax.rem(k // NX + NZ - z, NZ)]
+        return pltpu.make_async_copy(done.at[k], place, out_sem.at[k])
+
+    for p in range(pairs):
+        for k in (2 * p, 2 * p + 1):
+            for i in range(2):
+                part = here.at[p, i * feats : (i + 1) * feats, k % 2 * feats : (k % 2 + 1) * feats]
+                pltpu.make_async_copy(w.at[:, :feats], part, sem.at[2 * k + i]).wait()
+        both = dot(rows_in[...], here[p]).astype(BF)
+        for k in (2 * p, 2 * p + 1):
+            done[k] = both[:, k % 2 * feats : (k % 2 + 1) * feats]
+            leave(k).start()
     for k in range(blocks):
-        for copy in fetch(k):
-            copy.start()
-
-    def step(k, carry):
-        some = pl.ds(0, width)
-        pltpu.make_async_copy(w.at[:, some], here.at[k], sem.at[2 * k]).wait()
-        pltpu.make_async_copy(w_sib.at[:, some], here_sib.at[k], sem.at[2 * k + 1]).wait()
-        part = dot(att[:, :feats], here[k]) + dot(att[:, feats:], here_sib[k])
-        out[k % NX, lax.rem(k // NX + NZ - z, NZ)] = part.astype(out.dtype)
-        return carry
-
-    lax.fori_loop(0, blocks, step, 0)
-
-
-def out_partial(pos, att, w_out, w_sib):
+        leave(k).wait()
+
+
+def out_partial(pos, att, att_recv, w_out, w_sib):
     half, width = att.shape
     feats = width // NC
+    rows = NC * half
     blocks = NX * NZ
     return pl.pallas_call(
         out_kernel,
-        in_specs=[SMEM, VMEM, HBM, HBM],
-        out_specs=VMEM,
-        out_shape=struct((NX, NZ, half, width), BF),
-        scratch_shapes=[pltpu.VMEM((blocks, feats, width), BF)] * 2
-        + [pltpu.SemaphoreType.DMA((2 * blocks,))],
-        compiler_params=pltpu.CompilerParams(vmem_limit_bytes=40 * 2**20),
+        in_specs=[SMEM, VMEM, VMEM, HBM, HBM],
+        out_specs=HBM,
+        out_shape=struct((NX, NZ, rows, feats), BF),
+        scratch_shapes=[
+            pltpu.VMEM((rows, width), BF),
+            pltpu.VMEM((blocks // 2, width, 2 * feats), BF),
+            pltpu.VMEM((blocks, rows, feats), BF),
+            pltpu.SemaphoreType.DMA((2 * blocks,)),
+            pltpu.SemaphoreType.DMA((blocks,)),
+        ],
+        compiler_params=pltpu.CompilerParams(vmem_limit_bytes=50 * 2**20),
         cost_estimate=TINY,
-    )(pos, att, w_out, w_sib)
-
-
-def out_rank_kernel(pos, att, early, early_sib, out):
-    feats = early.shape[2] // PARTS
-    rank = dot_t(att[:, :feats], factor(early, 5))
-    rank = rank + dot_t(att[:, feats:], factor(early_sib, 5))
-    for j in range(NZ):
-        out[j] = rank.astype(BF)
-
-
-def out_rank_sum_kernel(pos, a, out):
-    total = a[0].astype(F32) + a[1].astype(F32) + a[2].astype(F32) + a[3].astype(F32)
-    for j in range(NX):
-        out[j] = total.astype(BF)
-
-
-def final_kernel(pos, a0, a1, a2, a3, r, early, early_sib, mine, send):
+    )(pos, att, att_recv, w_out, w_sib)
+
+
+def out_rank_kernel(pos, att, down_o, out):
+    out[...] = dot_t(att[...], down_o[...]).astype(BF)
+
+
+def add_kernel(pos, a0, a1, a2, a3, out):
+    total = a0[...].astype(F32) + a1[...].astype(F32)
+    out[...] = (total + a2[...].astype(F32) + a3[...].astype(F32)).astype(BF)
+
+
+def rank_rows_kernel(pos, a0, a1, a2, a3, own, s1, s2, s3, total):
+    total[...] = a0[...].astype(F32) + a1[...].astype(F32) + a2[...].astype(F32) + a3[...].astype(F32)
+    part = own.shape[0]
+    for d, out in enumerate((own, s1, s2, s3)):
+        rows = at(lax.rem(pos[1] + NX - d, NX) * part, part, part)
+        out[...] = total[rows, :].astype(BF)
+
+
+def rank_join_kernel(pos, a0, a1, a2, a3, out):
+    part = a0.shape[0]
+    for d, a in enumerate((a0, a1, a2, a3)):
+        out[at(lax.rem(pos[1] + d, NX) * part, part, part), :] = a[...]
+
+
+def final_kernel(pos, a0, a1, a2, a3, rank, rank_recv, up_o, out):
     c = pos[3]
-    feats = mine.shape[1]
-    rank = r[0].astype(F32) + r[1].astype(F32) + r[2].astype(F32) + r[3].astype(F32)
-    rank = rank.astype(BF)
-
-    def total(cols):
-        part = a0[:, cols].astype(F32) + a1[:, cols].astype(F32)
-        return part + a2[:, cols].astype(F32) + a3[:, cols].astype(F32)
-
-    low = dot(rank, factor(early, 6)) * SCALE
-    low_sib = dot(rank, factor(early_sib, 6)) * SCALE
-    mine[...] = (total(at(c * feats, feats)) + low).astype(BF)
-    send[...] = (total(at((1 - c) * feats, feats)) + low_sib).astype(BF)
-
-
-def join_kernel(pos, mine, recv, out):
-    c = pos[3]
-    half = mine.shape[0]
-    out[at(c * half, half), :] = mine[...]
-    out[at((1 - c) * half, half), :] = recv[...]
+    half = rank.shape[0]
+    for part, start in ((rank, c * half), (rank_recv, (1 - c) * half)):
+        rows = at(start, half)
+        total = a0[rows, :].astype(F32) + a1[rows, :].astype(F32)
+        total = total + a2[rows, :].astype(F32) + a3[rows, :].astype(F32)
+        out[rows, :] = (total + dot(part[...], up_o[...]) * SCALE).astype(BF)
 
 
 def body(
@@ -430,7 +440,18 @@
     own, *sends = call(kv_middle_kernel, four((half, 2 * HEAD_DIM)), (pos, *kv_x))
     kv_z = [own] + [from_z(s, d) for d, s in zip((1, 2, 3), sends)]
     pieces = swap_xz(pieces)
-    pieces, early_sib, w_out_now, kv_z = tie(pieces, early_sib, w_out, kv_z)
+    factors = call(
+        factors_kernel,
+        [
+            struct((n, NC * feats), BF),
+            struct((n, feats), BF),
+            struct((n, NC * feats), BF),
+            struct((n, feats), BF),
+        ],
+        (pos, early, early_sib),
+    )
+    pieces, factors, w_out_now, kv_z = tie(pieces, factors, w_out, kv_z)
+    up_q, up_kv, down_o, up_o = factors
     w_o_sib = from_core(w_out_now)
     pieces = call(rank_sum_kernel, struct(pieces.shape, BF), (pos, pieces))
     pieces = swap_xz(pieces)
@@ -438,30 +459,44 @@
     q_mine, q_send = query(pos, tok_all, w_query.reshape(NZ * NX * NC, feats, feats))
     q_recv = from_core(q_send)
     pieces, w_o_sib, q_recv = tie(pieces, w_o_sib, q_recv)
-    kv_mine = call(kv_final_kernel, struct((half, 2 * HEAD_DIM), BF), (pos, pieces, *kv_z, early))
+    kv_mine = call(kv_final_kernel, struct((half, 2 * HEAD_DIM), BF), (pos, pieces, *kv_z, up_kv))
 
     att = call(
         attend_kernel,
         struct((half, NC * feats), BF),
-        (pos, pieces, q_mine, q_recv, early, early_sib, kv_mine, from_core(kv_mine)),
+        (pos, pieces, q_mine, q_recv, up_q, kv_mine, from_core(kv_mine)),
         [vm((rows, 2 * HEAD_DIM), BF), vm((half, NC * feats), BF)],
     )
 
-    rank_o = call(out_rank_kernel, struct((NZ, half, n), BF), (pos, att, early, early_sib))
+    rank_o = call(out_rank_kernel, struct((half, n), BF), (pos, att, down_o))
     att, rank_o = tie(att, rank_o)
-    out = out_partial(pos, att, w_out, w_o_sib)
+    out = out_partial(pos, att, from_core(att), w_out, w_o_sib)
     out_x = lax.psum_scatter(
         out, "tensor", scatter_dimension=0, tiled=True, axis_index_groups=x_groups
     )
-    rank_o, _ = tie(rank_o, out)
-    rank_o = call(out_rank_sum_kernel, struct((NX, half, n), BF), (pos, swap_z(rank_o)))
-    rank_o = swap_x(rank_o)
+    own, *sends = call(
+        rank_rows_kernel,
+        [struct((half // NX, n), BF)] * NX,
+        (pos, rank_o, *[from_z(rank_o, d) for d in (1, 2, 3)]),
+        [vm((half, n), F32)],
+    )
+    part = call(
+        add_kernel,
+        struct((half // NX, n), BF),
+        (pos, own, *[from_x(s, d) for d, s in zip((1, 2, 3), sends)]),
+    )
+    rank_o = call(
+        rank_join_kernel,
+        struct((half, n), BF),
+        (pos, part, *[from_x(part, d) for d in (1, 2, 3)]),
+    )
     out_x = [out_x[0, i] for i in range(NZ)]
     out_z = [out_x[0]] + [from_z(out_x[NZ - d], d) for d in (1, 2, 3)]
-    mine, send = call(
-        final_kernel, [struct((half, feats), BF)] * 2, (pos, *out_z, rank_o, early, early_sib)
-    )
-    return call(join_kernel, struct((rows, feats), BF), (pos, mine, from_core(send)))
+    return call(
+        final_kernel,
+        struct((rows, feats), BF),
+        (pos, *out_z, rank_o, from_core(rank_o), up_o),
+    )
 
 
 def solution(mesh):

time: 188 us -> 184 us (0.979)
  blocking collectives: 17.2 us -> 0 us
  waiting for transfers between devices: 60.8 us -> 71 us
  starting transfers between devices: 59.4 us -> 61.8 us
  Pallas kernels: 24.2 us -> 22.1 us
    all_to_all x1 -> x0, blocking collectives: 17.2 us -> none  [swap_all(): return lax.all_to_all(a, axis, 0, 0, axis_index_groups=groups, tiled=True)]
    ppermute x6 -> x9, waiting for transfers between devices: 21.9 us -> 36.5 us  [from_z(): return lax.ppermute(a, 'tensor', tensor_perm(d, 0, 0))]
    reduce_scatter x1, waiting for transfers between devices: 9.68 us -> 0.01 us  [body(): lax.psum_scatter(out, 'tensor', scatter_dimension=0, tiled=True, axis_ind...]
    ppermute x3 -> x9, waiting for transfers between devices: 15.1 us -> 22.1 us  [from_x(): return lax.ppermute(a, 'tensor', tensor_perm(0, d, 0))]
    all_to_all x4 -> x3, starting transfers between devices: 26 us -> 19.8 us  [swap_all(): return lax.all_to_all(a, axis, 0, 0, axis_index_groups=groups, tiled=True)]
    ppermute x3 -> x9, starting transfers between devices: 3.59 us -> 9.19 us  [from_x(): return lax.ppermute(a, 'tensor', tensor_perm(0, d, 0))]
    ppermute x9 -> x10, starting transfers between devices: 9.42 us -> 13.8 us  [from_core(): return lax.ppermute(a, 'tensor', tensor_perm(0, 0, 1))]
    pallas_call x11 -> x13, Pallas kernels: 16.3 us -> 14.5 us  [call(): pl.pallas_call(kernel, out_shape=out_shape, in_specs=specs, out_specs=jax...]
  transfers between devices with their start and end apart: 24 -> 33, of which waited for: 13 -> 21; matrix products, arithmetic and copies ran while one was open for 1% -> 1% of each run, Pallas kernels for 6% -> 7%
where the time goes in v1:
time: 184 us; the launch traced here: 182 us
  waiting for transfers between devices  71 us (39%)
  starting transfers between devices  61.8 us (34%)
  Pallas kernels  22.1 us (12%)
  between operations  13.6 us (7%)
  local copies, waits for them, and re-layouts  12.4 us (7%)
    ppermute x9, waiting for transfers between devices, from_z(): return lax.ppermute(a, 'tensor', tensor_perm(d, 0, 0))  36.5 us
    ppermute x9, waiting for transfers between devices, from_x(): return lax.ppermute(a, 'tensor', tensor_perm(0, d, 0))  22.1 us
    all_to_all x3, starting transfers between devices, swap_all(): return lax.all_to_all(a, axis, 0, 0, axis_index_groups=groups, tiled=True)  19.8 us
    ppermute x9, starting transfers between devices, from_z(): return lax.ppermute(a, 'tensor', tensor_perm(d, 0, 0))  19 us
    pallas_call x13, Pallas kernels, call(): pl.pallas_call(kernel, out_shape=out_shape, in_specs=specs, out_specs=jax...  14.5 us
    ppermute x10, starting transfers between devices, from_core(): return lax.ppermute(a, 'tensor', tensor_perm(0, 0, 1))  13.8 us
    ppermute x9, starting transfers between devices, from_x(): return lax.ppermute(a, 'tensor', tensor_perm(0, d, 0))  9.19 us
    unnamed x34, local copies, waits for them, and re-layouts  8.41 us
  transfers between devices with their start and end apart: 33, of which 21 were waited for; matrix products, arithmetic and copies ran while one was open for 1% of the time, Pallas kernels for 7%

profile of v1, /device:TPU:25, one launch (start us, length us, event | category | flops | bytes accessed | tf_op | source)
XLA Modules:
  0.0 181.9 jit_solution(4000736073461542129)
XLA Ops:
  9.7 5.5 %all-to-all-start = ((bf16[8,64,1792]{2,1,0:T(8,128)(2,1)}), bf16[8,64,1792]{2,1,0:T(8,128)(2,1)S(1)}, u32[]{:S(2)}, u32[]{:S(2)}) async-start(bf16[8,64,1792]{2,1,0:T(8,128)(2,1)} %broadcast_in_dim.11), calls=%async_computation | async-start | bytes 3670016 | tf_op jit(solution)/shard_map/all_to_all | solution.py:51
  22.7 2.5 %collective-permute-start.3 = (bf16[128,1024]{1,0:T(8,128)(2,1)S(1)}, bf16[128,1024]{1,0:T(8,128)(2,1)S(1)}, u32[]{:S(2)}, u32[]{:S(2)}) collective-permute-start(bf16[128,1024]{1,0:T(8,128)(2,1)S(1)} %get-tuple-element.46), channel_id=1, source_target_pairs={{0,6},{1,7},{2,0},{3,1},{4,2},{5,3},{6,4},{7,5},{8,14},{9,15},{10,... | collective-permute-start | bytes 786440 | tf_op jit(solution)/shard_map/ppermute | solution.py:39
  26.3 9.6 %collective-permute-done.3.a1 = bf16[128,1024]{1,0:T(8,128)(2,1)S(1)} collective-permute-done((bf16[128,1024]{1,0:T(8,128)(2,1)S(1)}, bf16[128,1024]{1,0:T(8,128)(2,1)S(1)}, u32[]{:S(2)}, u32[]{:S(2)}) %collective-permute-start.3) | collective-permute-done | bytes 262176 | tf_op jit(solution)/shard_map/ppermute | solution.py:39
  35.8 5.5 %collective-permute-done.5.a3 = bf16[128,1024]{1,0:T(8,128)(2,1)S(1)} collective-permute-done((bf16[128,1024]{1,0:T(8,128)(2,1)S(1)}, bf16[128,1024]{1,0:T(8,128)(2,1)S(1)}, u32[]{:S(2)}, u32[]{:S(2)}) %collective-permute-start.5) | collective-permute-done | bytes 262176 | tf_op jit(solution)/shard_map/ppermute | solution.py:39
  43.3 2.5 %collective-permute-done.6.recv = bf16[128,1536]{1,0:T(8,128)(2,1)S(1)} collective-permute-done((bf16[128,1536]{1,0:T(8,128)(2,1)S(1)}, bf16[128,1536]{1,0:T(8,128)(2,1)S(1)}, u32[]{:S(2)}, u32[]{:S(2)}) %collective-permute-start.6) | collective-permute-done | bytes 393248 | tf_op jit(solution)/shard_map/ppermute | solution.py:35
  47.2 9.2 %all-to-all-start.1 = ((bf16[16,8,1536]{2,1,0:T(8,128)(2,1)}), bf16[16,8,1536]{2,1,0:T(8,128)(2,1)S(1)}, u32[]{:S(2)}, u32[]{:S(2)}) async-start(bf16[16,8,1536]{2,1,0:T(8,128)(2,1)} %shard_map.129), calls=%async_computation.1 | async-start | bytes 786432 | tf_op jit(solution)/shard_map/all_to_all | solution.py:51
  57.7 3.5 %collective-permute-start.8 = (bf16[128,256]{1,0:T(8,128)(2,1)S(1)}, bf16[128,256]{1,0:T(8,128)(2,1)S(1)}, u32[]{:S(2)}, u32[]{:S(2)}) collective-permute-start(bf16[128,256]{1,0:T(8,128)(2,1)S(1)} %get-tuple-element.61), channel_id=1, source_target_pairs={{0,24},{1,25},{2,26},{3,27},{4,28},{5,29},{6,30},{7,31},{8,0},{9,1... | collective-permute-start | bytes 196616 | tf_op jit(solution)/shard_map/ppermute | solution.py:43
  67.7 15.8 %collective-permute-done.8.a1 = bf16[128,256]{1,0:T(8,128)(2,1)S(1)} collective-permute-done((bf16[128,256]{1,0:T(8,128)(2,1)S(1)}, bf16[128,256]{1,0:T(8,128)(2,1)S(1)}, u32[]{:S(2)}, u32[]{:S(2)}) %collective-permute-start.8) | collective-permute-done | bytes 65568 | tf_op jit(solution)/shard_map/ppermute | solution.py:43
  85.4 5.5 %collective-permute-start.11 = (bf16[256,8192]{1,0:T(8,128)(2,1)}, bf16[256,8192]{1,0:T(8,128)(2,1)}, u32[]{:S(2)}, u32[]{:S(2)}) collective-permute-start(bf16[256,8192]{1,0:T(8,128)(2,1)} %w.1), channel_id=1, source_target_pairs={{0,1},{1,0},{2,3},{3,2},{4,5},{5,4},{6,7},{7,6},{8,9},{9,8},{10,11... | collective-permute-start | bytes 12582920 | tf_op jit(solution)/shard_map/ppermute | solution.py:35
  92.2 5.2 %all-to-all-start.2 = ((bf16[16,8,1536]{2,1,0:T(8,128)(2,1)}), bf16[16,8,1536]{2,1,0:T(8,128)(2,1)S(1)}, u32[]{:S(2)}, u32[]{:S(2)}) async-start(bf16[16,8,1536]{2,1,0:T(8,128)(2,1)} %shard_map.132), calls=%async_computation.2 | async-start | bytes 786432 | tf_op jit(solution)/shard_map/all_to_all | solution.py:51
  98.3 2.2 %copy-done = bf16[8192,256]{1,0:T(8,128)(2,1)S(1)} copy-done((bf16[8192,256]{1,0:T(8,128)(2,1)S(1)}, bf16[8192,256]{1,0:T(8,128)(2,1)}, u32[]{:S(2)}) %copy-start) | copy-done | bytes 4194328
  100.5 2.2 %copy-done.1 = bf16[8192,256]{1,0:T(8,128)(2,1)S(1)} copy-done((bf16[8192,256]{1,0:T(8,128)(2,1)S(1)}, bf16[8192,256]{1,0:T(8,128)(2,1)}, u32[]{:S(2)}) %copy-start.1) | copy-done | bytes 4194328
  102.7 2.4 %shard_map.133 = (f32[128,256]{1,0:T(8,128)S(1)}, f32[128,256]{1,0:T(8,128)S(1)}) custom-call(s32[4]{0:T(128)S(1)} %pad_add_fusion.refs_0_.pos, bf16[32,256,256]{2,1,0:T(8,128)(2,1)S(1)} %bitcast.21, bf16[32,256,256]{2,1,0:T(8,128)(2,1)S(1)} %bitcast.20), custom_call_target="tpu_custom_call" | custom-call | flops 1000 | bytes 1000 | tf_op jit(solution)/shard_map/pallas_call | solution.py:264
  105.4 5.0 %all-to-all-done.2.pieces = bf16[16,8,1536]{2,1,0:T(8,128)(2,1)S(1)} async-done(((bf16[16,8,1536]{2,1,0:T(8,128)(2,1)}), bf16[16,8,1536]{2,1,0:T(8,128)(2,1)S(1)}, u32[]{:S(2)}, u32[]{:S(2)}) %all-to-all-start.2) | async-done | bytes 393248 | tf_op jit(solution)/shard_map/all_to_all | solution.py:51
  117.8 5.2 %shard_map.137 = bf16[4,4,256,256]{3,2,1,0:T(8,128)(2,1)} custom-call(s32[4]{0:T(128)S(1)} %pad_add_fusion.refs_0_.pos, bf16[128,512]{1,0:T(8,128)(2,1)S(1)} %shard_map.135.att, bf16[128,512]{1,0:T(8,128)(2,1)S(1)} %collective-permute-done.14.att_recv, bf16[256,8192]{1,0:T(8,128)(2,1)} %w.1, bf16[256,8192]{1,0:T(8,128)(2,1)} %collective-permute-done.11.w_sib), custom_call_target="tpu_custom_call" | custom-call | flops 1000 | bytes 1000 | tf_op jit(solution)/shard_map/pallas_call | solution.py:326
  123.4 3.1 %collective-permute-start.19 = (bf16[128,512]{1,0:T(8,128)(2,1)S(1)}, bf16[128,512]{1,0:T(8,128)(2,1)S(1)}, u32[]{:S(2)}, u32[]{:S(2)}) collective-permute-start(bf16[128,512]{1,0:T(8,128)(2,1)S(1)} %shard_map.136.a0), channel_id=1, source_target_pairs={{0,16},{1,17},{2,18},{3,19},{4,20},{5,21},{6,22},{7,23},{8,24},{9,... | collective-permute-start | bytes 393224 | tf_op jit(solution)/shard_map/ppermute | solution.py:43
  127.5 2.5 %collective-permute-done.20.a3 = bf16[128,512]{1,0:T(8,128)(2,1)S(1)} collective-permute-done((bf16[128,512]{1,0:T(8,128)(2,1)S(1)}, bf16[128,512]{1,0:T(8,128)(2,1)S(1)}, u32[]{:S(2)}, u32[]{:S(2)}) %collective-permute-start.20) | collective-permute-done | bytes 131104 | tf_op jit(solution)/shard_map/ppermute | solution.py:43
  130.0 2.8 %collective-permute-done.19.a2 = bf16[128,512]{1,0:T(8,128)(2,1)S(1)} collective-permute-done((bf16[128,512]{1,0:T(8,128)(2,1)S(1)}, bf16[128,512]{1,0:T(8,128)(2,1)S(1)}, u32[]{:S(2)}, u32[]{:S(2)}) %collective-permute-start.19) | collective-permute-done | bytes 131104 | tf_op jit(solution)/shard_map/ppermute | solution.py:43
  132.8 5.4 %collective-permute-done.18.a1 = bf16[128,512]{1,0:T(8,128)(2,1)S(1)} collective-permute-done((bf16[128,512]{1,0:T(8,128)(2,1)S(1)}, bf16[128,512]{1,0:T(8,128)(2,1)S(1)}, u32[]{:S(2)}, u32[]{:S(2)}) %collective-permute-start.18) | collective-permute-done | bytes 131104 | tf_op jit(solution)/shard_map/ppermute | solution.py:43
  152.5 3.0 %collective-permute-start.27 = (bf16[128,512]{1,0:T(8,128)(2,1)S(1)}, bf16[128,512]{1,0:T(8,128)(2,1)S(1)}, u32[]{:S(2)}, u32[]{:S(2)}) collective-permute-start(bf16[128,512]{1,0:T(8,128)(2,1)S(1)} %shard_map.140.rank), channel_id=1, source_target_pairs={{0,1},{1,0},{2,3},{3,2},{4,5},{5,4},{6,7},{7,6},{8,9},{9,8},{10,11... | collective-permute-start | bytes 393224 | tf_op jit(solution)/shard_map/ppermute | solution.py:35
  156.7 2.6 %collective-permute-start.17 = (bf16[256,256]{1,0:T(8,128)(2,1)S(1)}, bf16[256,256]{1,0:T(8,128)(2,1)S(1)}, u32[]{:S(2)}, u32[]{:S(2)}) collective-permute-start(bf16[256,256]{1,0:T(8,128)(2,1)S(1)} %get-tuple-element.85), channel_id=1, source_target_pairs={{0,8},{1,9},{2,10},{3,11},{4,12},{5,13},{6,14},{7,15},{8,16},{9,17... | collective-permute-start | bytes 393224 | tf_op jit(solution)/shard_map/ppermute | solution.py:43
  160.5 3.1 %collective-permute-start.15 = (bf16[256,256]{1,0:T(8,128)(2,1)S(1)}, bf16[256,256]{1,0:T(8,128)(2,1)S(1)}, u32[]{:S(2)}, u32[]{:S(2)}) collective-permute-start(bf16[256,256]{1,0:T(8,128)(2,1)S(1)} %get-tuple-element.87), channel_id=1, source_target_pairs={{0,24},{1,25},{2,26},{3,27},{4,28},{5,29},{6,30},{7,31},{8,0},{9,1... | collective-permute-start | bytes 393224 | tf_op jit(solution)/shard_map/ppermute | solution.py:43
  165.4 5.4 %collective-permute-done.16.a2 = bf16[256,256]{1,0:T(8,128)(2,1)S(1)} collective-permute-done((bf16[256,256]{1,0:T(8,128)(2,1)S(1)}, bf16[256,256]{1,0:T(8,128)(2,1)S(1)}, u32[]{:S(2)}, u32[]{:S(2)}) %collective-permute-start.16) | collective-permute-done | bytes 131104 | tf_op jit(solution)/shard_map/ppermute | solution.py:43
  170.8 2.8 %collective-permute-done.15.a1 = bf16[256,256]{1,0:T(8,128)(2,1)S(1)} collective-permute-done((bf16[256,256]{1,0:T(8,128)(2,1)S(1)}, bf16[256,256]{1,0:T(8,128)(2,1)S(1)}, u32[]{:S(2)}, u32[]{:S(2)}) %collective-permute-start.15) | collective-permute-done | bytes 131104 | tf_op jit(solution)/shard_map/ppermute | solution.py:43
  (99 shorter events, 56.1 us)
Async XLA Ops:
  9.7 31.7 %all-to-all-start = ((bf16[8,64,1792]{2,1,0:T(8,128)(2,1)}), bf16[8,64,1792]{2,1,0:T(8,128)(2,1)S(1)}, u32[]{:S(2)}, u32[]{:S(2)}) async-start(bf16[8,64,1792]{2,1,0:T(8,128)(2,1)} %broadcast_in_dim.11), calls=%async_computation | async-start | bytes 3670016 | tf_op jit(solution)/shard_map/all_to_all | solution.py:51
  15.1 83.1 %all-gather.3.cloned.1.call-start = ((), (), s32[]{:S(2)}) async-start(), calls=%async_computation.5 | async-start | bytes 4325376 | tf_op jit(solution)/shard_map/all_gather | solution.py:413
  22.7 13.2 %collective-permute-start.3 = (bf16[128,1024]{1,0:T(8,128)(2,1)S(1)}, bf16[128,1024]{1,0:T(8,128)(2,1)S(1)}, u32[]{:S(2)}, u32[]{:S(2)}) collective-permute-start(bf16[128,1024]{1,0:T(8,128)(2,1)S(1)} %get-tuple-element.46), channel_id=1, source_target_pairs={{0,6},{1,7},{2,0},{3,1},{4,2},{5,3},{6,4},{7,5},{8,14},{9,15},{10,... | collective-permute-start | bytes 786440 | tf_op jit(solution)/shard_map/ppermute | solution.py:39
  25.1 10.7 %collective-permute-start.4 = (bf16[128,1024]{1,0:T(8,128)(2,1)S(1)}, bf16[128,1024]{1,0:T(8,128)(2,1)S(1)}, u32[]{:S(2)}, u32[]{:S(2)}) collective-permute-start(bf16[128,1024]{1,0:T(8,128)(2,1)S(1)} %get-tuple-element.47), channel_id=1, source_target_pairs={{0,4},{1,5},{2,6},{3,7},{4,0},{5,1},{6,2},{7,3},{8,12},{9,13},{10,... | collective-permute-start | bytes 786440 | tf_op jit(solution)/shard_map/ppermute | solution.py:39
  25.7 15.7 %collective-permute-start.5 = (bf16[128,1024]{1,0:T(8,128)(2,1)S(1)}, bf16[128,1024]{1,0:T(8,128)(2,1)S(1)}, u32[]{:S(2)}, u32[]{:S(2)}) collective-permute-start(bf16[128,1024]{1,0:T(8,128)(2,1)S(1)} %get-tuple-element.48), channel_id=1, source_target_pairs={{0,2},{1,3},{2,4},{3,5},{4,6},{5,7},{6,0},{7,1},{8,10},{9,11},{10,... | collective-permute-start | bytes 786440 | tf_op jit(solution)/shard_map/ppermute | solution.py:39
  41.4 24.0 %collective-permute-start.7 = (bf16[8,64,1792]{2,1,0:T(8,128)(2,1)S(1)}, bf16[8,64,1792]{2,1,0:T(8,128)(2,1)}, u32[]{:S(2)}, u32[]{:S(2)}) collective-permute-start(bf16[8,64,1792]{2,1,0:T(8,128)(2,1)S(1)} %all-to-all-done.refs_2_.early), channel_id=1, source_target_pairs={{0,1},{1,0},{2,3},{3,2},{4,5},{5,4},{6,7},{7,6},{8,9},{9,8},{10,11... | collective-permute-start | bytes 5505032 | tf_op jit(solution)/shard_map/ppermute | solution.py:35
  47.2 38.2 %all-to-all-start.1 = ((bf16[16,8,1536]{2,1,0:T(8,128)(2,1)}), bf16[16,8,1536]{2,1,0:T(8,128)(2,1)S(1)}, u32[]{:S(2)}, u32[]{:S(2)}) async-start(bf16[16,8,1536]{2,1,0:T(8,128)(2,1)} %shard_map.129), calls=%async_computation.1 | async-start | bytes 786432 | tf_op jit(solution)/shard_map/all_to_all | solution.py:51
  57.7 25.8 %collective-permute-start.8 = (bf16[128,256]{1,0:T(8,128)(2,1)S(1)}, bf16[128,256]{1,0:T(8,128)(2,1)S(1)}, u32[]{:S(2)}, u32[]{:S(2)}) collective-permute-start(bf16[128,256]{1,0:T(8,128)(2,1)S(1)} %get-tuple-element.61), channel_id=1, source_target_pairs={{0,24},{1,25},{2,26},{3,27},{4,28},{5,29},{6,30},{7,31},{8,0},{9,1... | collective-permute-start | bytes 196616 | tf_op jit(solution)/shard_map/ppermute | solution.py:43
  61.2 22.9 %collective-permute-start.9 = (bf16[128,256]{1,0:T(8,128)(2,1)S(1)}, bf16[128,256]{1,0:T(8,128)(2,1)S(1)}, u32[]{:S(2)}, u32[]{:S(2)}) collective-permute-start(bf16[128,256]{1,0:T(8,128)(2,1)S(1)} %get-tuple-element.62), channel_id=1, source_target_pairs={{0,16},{1,17},{2,18},{3,19},{4,20},{5,21},{6,22},{7,23},{8,24},{9,... | collective-permute-start | bytes 196616 | tf_op jit(solution)/shard_map/ppermute | solution.py:43
  63.3 21.5 %collective-permute-start.10 = (bf16[128,256]{1,0:T(8,128)(2,1)S(1)}, bf16[128,256]{1,0:T(8,128)(2,1)S(1)}, u32[]{:S(2)}, u32[]{:S(2)}) collective-permute-start(bf16[128,256]{1,0:T(8,128)(2,1)S(1)} %get-tuple-element.63), channel_id=1, source_target_pairs={{0,8},{1,9},{2,10},{3,11},{4,12},{5,13},{6,14},{7,15},{8,16},{9,17... | collective-permute-start | bytes 196616 | tf_op jit(solution)/shard_map/ppermute | solution.py:43
  85.4 25.0 %collective-permute-start.11 = (bf16[256,8192]{1,0:T(8,128)(2,1)}, bf16[256,8192]{1,0:T(8,128)(2,1)}, u32[]{:S(2)}, u32[]{:S(2)}) collective-permute-start(bf16[256,8192]{1,0:T(8,128)(2,1)} %w.1), channel_id=1, source_target_pairs={{0,1},{1,0},{2,3},{3,2},{4,5},{5,4},{6,7},{7,6},{8,9},{9,8},{10,11... | collective-permute-start | bytes 12582920 | tf_op jit(solution)/shard_map/ppermute | solution.py:35
  92.2 18.1 %all-to-all-start.2 = ((bf16[16,8,1536]{2,1,0:T(8,128)(2,1)}), bf16[16,8,1536]{2,1,0:T(8,128)(2,1)S(1)}, u32[]{:S(2)}, u32[]{:S(2)}) async-start(bf16[16,8,1536]{2,1,0:T(8,128)(2,1)} %shard_map.132), calls=%async_computation.2 | async-start | bytes 786432 | tf_op jit(solution)/shard_map/all_to_all | solution.py:51
  97.4 58.2 %reduce-scatter.2.cloned.1.call-start = ((), (), s32[]{:S(2)}) async-start(), calls=%async_computation.4 | async-start | bytes 2621440 | tf_op jit(solution)/shard_map/reduce_scatter | solution.py:474
  105.1 5.3 %collective-permute-start.12 = (f32[128,256]{1,0:T(8,128)S(1)}, f32[128,256]{1,0:T(8,128)S(1)}, u32[]{:S(2)}, u32[]{:S(2)}) collective-permute-start(f32[128,256]{1,0:T(8,128)S(1)} %get-tuple-element.66), channel_id=1, source_target_pairs={{0,1},{1,0},{2,3},{3,2},{4,5},{5,4},{6,7},{7,6},{8,9},{9,8},{10,11... | collective-permute-start | bytes 393224 | tf_op jit(solution)/shard_map/ppermute | solution.py:35
  123.1 6.9 %collective-permute-start.20 = (bf16[128,512]{1,0:T(8,128)(2,1)S(1)}, bf16[128,512]{1,0:T(8,128)(2,1)S(1)}, u32[]{:S(2)}, u32[]{:S(2)}) collective-permute-start(bf16[128,512]{1,0:T(8,128)(2,1)S(1)} %shard_map.136.a0), channel_id=1, source_target_pairs={{0,8},{1,9},{2,10},{3,11},{4,12},{5,13},{6,14},{7,15},{8,16},{9,17... | collective-permute-start | bytes 393224 | tf_op jit(solution)/shard_map/ppermute | solution.py:43
  123.4 9.4 %collective-permute-start.19 = (bf16[128,512]{1,0:T(8,128)(2,1)S(1)}, bf16[128,512]{1,0:T(8,128)(2,1)S(1)}, u32[]{:S(2)}, u32[]{:S(2)}) collective-permute-start(bf16[128,512]{1,0:T(8,128)(2,1)S(1)} %shard_map.136.a0), channel_id=1, source_target_pairs={{0,16},{1,17},{2,18},{3,19},{4,20},{5,21},{6,22},{7,23},{8,24},{9,... | collective-permute-start | bytes 393224 | tf_op jit(solution)/shard_map/ppermute | solution.py:43
  126.5 11.7 %collective-permute-start.18 = (bf16[128,512]{1,0:T(8,128)(2,1)S(1)}, bf16[128,512]{1,0:T(8,128)(2,1)S(1)}, u32[]{:S(2)}, u32[]{:S(2)}) collective-permute-start(bf16[128,512]{1,0:T(8,128)(2,1)S(1)} %shard_map.136.a0), channel_id=1, source_target_pairs={{0,24},{1,25},{2,26},{3,27},{4,28},{5,29},{6,30},{7,31},{8,0},{9,1... | collective-permute-start | bytes 393224 | tf_op jit(solution)/shard_map/ppermute | solution.py:43
  139.9 5.1 %collective-permute-start.22 = (bf16[32,512]{1,0:T(8,128)(2,1)S(1)}, bf16[32,512]{1,0:T(8,128)(2,1)S(1)}, u32[]{:S(2)}, u32[]{:S(2)}) collective-permute-start(bf16[32,512]{1,0:T(8,128)(2,1)S(1)} %get-tuple-element.82), channel_id=1, source_target_pairs={{0,4},{1,5},{2,6},{3,7},{4,0},{5,1},{6,2},{7,3},{8,12},{9,13},{10,... | collective-permute-start | bytes 98312 | tf_op jit(solution)/shard_map/ppermute | solution.py:39
  140.6 5.8 %collective-permute-start.23 = (bf16[32,512]{1,0:T(8,128)(2,1)S(1)}, bf16[32,512]{1,0:T(8,128)(2,1)S(1)}, u32[]{:S(2)}, u32[]{:S(2)}) collective-permute-start(bf16[32,512]{1,0:T(8,128)(2,1)S(1)} %get-tuple-element.83), channel_id=1, source_target_pairs={{0,2},{1,3},{2,4},{3,5},{4,6},{5,7},{6,0},{7,1},{8,10},{9,11},{10,... | collective-permute-start | bytes 98312 | tf_op jit(solution)/shard_map/ppermute | solution.py:39
  147.1 4.7 %collective-permute-start.25 = (bf16[32,512]{1,0:T(8,128)(2,1)S(1)}, bf16[32,512]{1,0:T(8,128)(2,1)S(1)}, u32[]{:S(2)}, u32[]{:S(2)}) collective-permute-start(bf16[32,512]{1,0:T(8,128)(2,1)S(1)} %shard_map.139.a0), channel_id=1, source_target_pairs={{0,4},{1,5},{2,6},{3,7},{4,0},{5,1},{6,2},{7,3},{8,12},{9,13},{10,... | collective-permute-start | bytes 98312 | tf_op jit(solution)/shard_map/ppermute | solution.py:39
  152.5 11.1 %collective-permute-start.27 = (bf16[128,512]{1,0:T(8,128)(2,1)S(1)}, bf16[128,512]{1,0:T(8,128)(2,1)S(1)}, u32[]{:S(2)}, u32[]{:S(2)}) collective-permute-start(bf16[128,512]{1,0:T(8,128)(2,1)S(1)} %shard_map.140.rank), channel_id=1, source_target_pairs={{0,1},{1,0},{2,3},{3,2},{4,5},{5,4},{6,7},{7,6},{8,9},{9,8},{10,11... | collective-permute-start | bytes 393224 | tf_op jit(solution)/shard_map/ppermute | solution.py:35
  156.7 8.7 %collective-permute-start.17 = (bf16[256,256]{1,0:T(8,128)(2,1)S(1)}, bf16[256,256]{1,0:T(8,128)(2,1)S(1)}, u32[]{:S(2)}, u32[]{:S(2)}) collective-permute-start(bf16[256,256]{1,0:T(8,128)(2,1)S(1)} %get-tuple-element.85), channel_id=1, source_target_pairs={{0,8},{1,9},{2,10},{3,11},{4,12},{5,13},{6,14},{7,15},{8,16},{9,17... | collective-permute-start | bytes 393224 | tf_op jit(solution)/shard_map/ppermute | solution.py:43
  159.2 11.6 %collective-permute-start.16 = (bf16[256,256]{1,0:T(8,128)(2,1)S(1)}, bf16[256,256]{1,0:T(8,128)(2,1)S(1)}, u32[]{:S(2)}, u32[]{:S(2)}) collective-permute-start(bf16[256,256]{1,0:T(8,128)(2,1)S(1)} %get-tuple-element.86), channel_id=1, source_target_pairs={{0,16},{1,17},{2,18},{3,19},{4,20},{5,21},{6,22},{7,23},{8,24},{9,... | collective-permute-start | bytes 393224 | tf_op jit(solution)/shard_map/ppermute | solution.py:43
  160.5 13.1 %collective-permute-start.15 = (bf16[256,256]{1,0:T(8,128)(2,1)S(1)}, bf16[256,256]{1,0:T(8,128)(2,1)S(1)}, u32[]{:S(2)}, u32[]{:S(2)}) collective-permute-start(bf16[256,256]{1,0:T(8,128)(2,1)S(1)} %get-tuple-element.87), channel_id=1, source_target_pairs={{0,24},{1,25},{2,26},{3,27},{4,28},{5,29},{6,30},{7,31},{8,0},{9,1... | collective-permute-start | bytes 393224 | tf_op jit(solution)/shard_map/ppermute | solution.py:43
  (26 other events, 138.8 us)
Sparse Core Ops, SparseCore 0:
  18.5 79.6 all-gather.2
  123.2 28.7 reduce-scatter.1

commit v2 on v1

--- a/solution.py
+++ b/solution.py
@@ -421,7 +421,7 @@
         held=(1, 3, 4),
     )
     kv_x = [own] + [from_x(s, d) for d, s in zip((1, 2, 3), sends)]
-    early, kv_x = tie(early, kv_x)
+    early, kv_x[0] = tie(early, kv_x[0])
 
     mine, send = call(
         rank_kernel,
@@ -437,6 +437,7 @@
         (pos, mine, from_core(send)),
     )
     early_sib = from_core(early)
+    pieces, kv_x = tie(pieces, kv_x)
     own, *sends = call(kv_middle_kernel, four((half, 2 * HEAD_DIM)), (pos, *kv_x))
     kv_z = [own] + [from_z(s, d) for d, s in zip((1, 2, 3), sends)]
     pieces = swap_xz(pieces)

time: 184 us -> 197 us (1.071)
  waiting for transfers between devices: 71 us -> 78.9 us
  starting transfers between devices: 61.8 us -> 65.4 us
  local copies, waits for them, and re-layouts: 12.4 us -> 14.6 us
    all_to_all x3, waiting for transfers between devices: 4.97 us -> 17.1 us  [swap_all(): return lax.all_to_all(a, axis, 0, 0, axis_index_groups=groups, tiled=True)]
    ppermute x9, starting transfers between devices: 9.19 us -> 12.8 us  [from_x(): return lax.ppermute(a, 'tensor', tensor_perm(0, d, 0))]
    ppermute x10, waiting for transfers between devices: 5.91 us -> 3.41 us  [from_core(): return lax.ppermute(a, 'tensor', tensor_perm(0, 0, 1))]
    unnamed x34 -> x40, local copies, waits for them, and re-layouts: 8.41 us -> 10.6 us
  transfers between devices with their start and end apart: 33 -> 33, of which waited for: 21 -> 21; matrix products, arithmetic and copies ran while one was open for 1% -> 1% of each run, Pallas kernels for 7% -> 6%
where the time goes in v2:
time: 197 us; the launch traced here: 196 us
  waiting for transfers between devices  78.9 us (40%)
  starting transfers between devices  65.4 us (33%)
  Pallas kernels  22.1 us (11%)
  local copies, waits for them, and re-layouts  14.6 us (7%)
  between operations  13.7 us (7%)
    ppermute x9, waiting for transfers between devices, from_z(): return lax.ppermute(a, 'tensor', tensor_perm(d, 0, 0))  37.3 us
    ppermute x9, waiting for transfers between devices, from_x(): return lax.ppermute(a, 'tensor', tensor_perm(0, d, 0))  20.3 us
    all_to_all x3, starting transfers between devices, swap_all(): return lax.all_to_all(a, axis, 0, 0, axis_index_groups=groups, tiled=True)  20.2 us
    ppermute x9, starting transfers between devices, from_z(): return lax.ppermute(a, 'tensor', tensor_perm(d, 0, 0))  19.7 us
    all_to_all x3, waiting for transfers between devices, swap_all(): return lax.all_to_all(a, axis, 0, 0, axis_index_groups=groups, tiled=True)  17.1 us
    pallas_call x13, Pallas kernels, call(): pl.pallas_call(kernel, out_shape=out_shape, in_specs=specs, out_specs=jax...  14.6 us
    ppermute x9, starting transfers between devices, from_x(): return lax.ppermute(a, 'tensor', tensor_perm(0, d, 0))  12.8 us
    ppermute x10, starting transfers between devices, from_core(): return lax.ppermute(a, 'tensor', tensor_perm(0, 0, 1))  12.7 us
  transfers between devices with their start and end apart: 33, of which 21 were waited for; matrix products, arithmetic and copies ran while one was open for 1% of the time, Pallas kernels for 6%

profile of v2, /device:TPU:25, one launch (start us, length us, event | category | flops | bytes accessed | tf_op | source)
XLA Modules:
  0.0 195.6 jit_solution(17606853431569880331)
XLA Ops:
  9.6 5.5 %all-to-all-start = ((bf16[8,64,1792]{2,1,0:T(8,128)(2,1)}), bf16[8,64,1792]{2,1,0:T(8,128)(2,1)S(1)}, u32[]{:S(2)}, u32[]{:S(2)}) async-start(bf16[8,64,1792]{2,1,0:T(8,128)(2,1)} %broadcast_in_dim.11), calls=%async_computation | async-start | bytes 3670016 | tf_op jit(solution)/shard_map/all_to_all | solution.py:51
  24.8 12.1 %all-to-all-done.refs_2_.early = bf16[8,64,1792]{2,1,0:T(8,128)(2,1)S(1)} async-done(((bf16[8,64,1792]{2,1,0:T(8,128)(2,1)}), bf16[8,64,1792]{2,1,0:T(8,128)(2,1)S(1)}, u32[]{:S(2)}, u32[]{:S(2)}) %all-to-all-start) | async-done | bytes 1835040 | tf_op jit(solution)/shard_map/all_to_all | solution.py:51
  36.9 3.3 %collective-permute-start.7 = (bf16[8,64,1792]{2,1,0:T(8,128)(2,1)S(1)}, bf16[8,64,1792]{2,1,0:T(8,128)(2,1)}, u32[]{:S(2)}, u32[]{:S(2)}) collective-permute-start(bf16[8,64,1792]{2,1,0:T(8,128)(2,1)S(1)} %all-to-all-done.refs_2_.early), channel_id=1, source_target_pairs={{0,1},{1,0},{2,3},{3,2},{4,5},{5,4},{6,7},{7,6},{8,9},{9,8},{10,11... | collective-permute-start | bytes 5505032 | tf_op jit(solution)/shard_map/ppermute | solution.py:35
  41.6 2.6 %collective-permute-start.4 = (bf16[128,1024]{1,0:T(8,128)(2,1)}, bf16[128,1024]{1,0:T(8,128)(2,1)S(1)}, u32[]{:S(2)}, u32[]{:S(2)}) collective-permute-start(bf16[128,1024]{1,0:T(8,128)(2,1)} %copy-done.19), channel_id=1, source_target_pairs={{0,6},{1,7},{2,0},{3,1},{4,2},{5,3},{6,4},{7,5},{8,14},{9,15},{10,... | collective-permute-start | bytes 786440 | tf_op jit(solution)/shard_map/ppermute | solution.py:39
  46.7 4.3 %collective-permute-done.4.a1 = bf16[128,1024]{1,0:T(8,128)(2,1)S(1)} collective-permute-done((bf16[128,1024]{1,0:T(8,128)(2,1)}, bf16[128,1024]{1,0:T(8,128)(2,1)S(1)}, u32[]{:S(2)}, u32[]{:S(2)}) %collective-permute-start.4) | collective-permute-done | bytes 262176 | tf_op jit(solution)/shard_map/ppermute | solution.py:39
  51.0 2.7 %collective-permute-done.5.a2 = bf16[128,1024]{1,0:T(8,128)(2,1)S(1)} collective-permute-done((bf16[128,1024]{1,0:T(8,128)(2,1)}, bf16[128,1024]{1,0:T(8,128)(2,1)S(1)}, u32[]{:S(2)}, u32[]{:S(2)}) %collective-permute-start.5) | collective-permute-done | bytes 262176 | tf_op jit(solution)/shard_map/ppermute | solution.py:39
  53.7 6.3 %collective-permute-done.6.a3 = bf16[128,1024]{1,0:T(8,128)(2,1)S(1)} collective-permute-done((bf16[128,1024]{1,0:T(8,128)(2,1)}, bf16[128,1024]{1,0:T(8,128)(2,1)S(1)}, u32[]{:S(2)}, u32[]{:S(2)}) %collective-permute-start.6) | collective-permute-done | bytes 262176 | tf_op jit(solution)/shard_map/ppermute | solution.py:39
  60.0 8.4 %all-to-all-start.1 = ((bf16[16,8,1536]{2,1,0:T(8,128)(2,1)}), bf16[16,8,1536]{2,1,0:T(8,128)(2,1)S(1)}, u32[]{:S(2)}, u32[]{:S(2)}) async-start(bf16[16,8,1536]{2,1,0:T(8,128)(2,1)} %shard_map.129), calls=%async_computation.1 | async-start | bytes 786432 | tf_op jit(solution)/shard_map/all_to_all | solution.py:51
  69.7 3.5 %collective-permute-start.8 = (bf16[128,256]{1,0:T(8,128)(2,1)S(1)}, bf16[128,256]{1,0:T(8,128)(2,1)S(1)}, u32[]{:S(2)}, u32[]{:S(2)}) collective-permute-start(bf16[128,256]{1,0:T(8,128)(2,1)S(1)} %get-tuple-element.65), channel_id=1, source_target_pairs={{0,24},{1,25},{2,26},{3,27},{4,28},{5,29},{6,30},{7,31},{8,0},{9,1... | collective-permute-start | bytes 196616 | tf_op jit(solution)/shard_map/ppermute | solution.py:43
  79.8 3.5 %collective-permute-done.8.a1 = bf16[128,256]{1,0:T(8,128)(2,1)S(1)} collective-permute-done((bf16[128,256]{1,0:T(8,128)(2,1)S(1)}, bf16[128,256]{1,0:T(8,128)(2,1)S(1)}, u32[]{:S(2)}, u32[]{:S(2)}) %collective-permute-start.8) | collective-permute-done | bytes 65568 | tf_op jit(solution)/shard_map/ppermute | solution.py:43
  83.9 10.8 %collective-permute-done.9.a2 = bf16[128,256]{1,0:T(8,128)(2,1)S(1)} collective-permute-done((bf16[128,256]{1,0:T(8,128)(2,1)S(1)}, bf16[128,256]{1,0:T(8,128)(2,1)S(1)}, u32[]{:S(2)}, u32[]{:S(2)}) %collective-permute-start.9) | collective-permute-done | bytes 65568 | tf_op jit(solution)/shard_map/ppermute | solution.py:43
  98.1 6.3 %all-to-all-start.2 = ((bf16[16,8,1536]{2,1,0:T(8,128)(2,1)}), bf16[16,8,1536]{2,1,0:T(8,128)(2,1)S(1)}, u32[]{:S(2)}, u32[]{:S(2)}) async-start(bf16[16,8,1536]{2,1,0:T(8,128)(2,1)} %shard_map.132), calls=%async_computation.2 | async-start | bytes 786432 | tf_op jit(solution)/shard_map/all_to_all | solution.py:51
  111.7 5.0 %all-to-all-done.2.pieces = bf16[16,8,1536]{2,1,0:T(8,128)(2,1)S(1)} async-done(((bf16[16,8,1536]{2,1,0:T(8,128)(2,1)}), bf16[16,8,1536]{2,1,0:T(8,128)(2,1)S(1)}, u32[]{:S(2)}, u32[]{:S(2)}) %all-to-all-start.2) | async-done | bytes 393248 | tf_op jit(solution)/shard_map/all_to_all | solution.py:51
  117.6 2.4 %collective-permute-start.13 = (bf16[128,256]{1,0:T(8,128)(2,1)S(1)}, bf16[128,256]{1,0:T(8,128)(2,1)S(1)}, u32[]{:S(2)}, u32[]{:S(2)}) collective-permute-start(bf16[128,256]{1,0:T(8,128)(2,1)S(1)} %shard_map.134.kv_mine), channel_id=1, source_target_pairs={{0,1},{1,0},{2,3},{3,2},{4,5},{5,4},{6,7},{7,6},{8,9},{9,8},{10,11... | collective-permute-start | bytes 196616 | tf_op jit(solution)/shard_map/ppermute | solution.py:35
  124.5 5.2 %shard_map.137 = bf16[4,4,256,256]{3,2,1,0:T(8,128)(2,1)} custom-call(s32[4]{0:T(128)S(1)} %pad_add_fusion.refs_0_.pos, bf16[128,512]{1,0:T(8,128)(2,1)S(1)} %shard_map.135.att, bf16[128,512]{1,0:T(8,128)(2,1)S(1)} %collective-permute-done.14.att_recv, bf16[256,8192]{1,0:T(8,128)(2,1)} %w.1, bf16[256,8192]{1,0:T(8,128)(2,1)} %collective-permute-done.11.w_sib), custom_call_target="tpu_custom_call" | custom-call | flops 1000 | bytes 1000 | tf_op jit(solution)/shard_map/pallas_call | solution.py:326
  129.9 5.7 %collective-permute-start.19 = (bf16[128,512]{1,0:T(8,128)(2,1)S(1)}, bf16[128,512]{1,0:T(8,128)(2,1)S(1)}, u32[]{:S(2)}, u32[]{:S(2)}) collective-permute-start(bf16[128,512]{1,0:T(8,128)(2,1)S(1)} %shard_map.136.a0), channel_id=1, source_target_pairs={{0,16},{1,17},{2,18},{3,19},{4,20},{5,21},{6,22},{7,23},{8,24},{9,... | collective-permute-start | bytes 393224 | tf_op jit(solution)/shard_map/ppermute | solution.py:43
  137.1 8.2 %collective-permute-done.19.a2 = bf16[128,512]{1,0:T(8,128)(2,1)S(1)} collective-permute-done((bf16[128,512]{1,0:T(8,128)(2,1)S(1)}, bf16[128,512]{1,0:T(8,128)(2,1)S(1)}, u32[]{:S(2)}, u32[]{:S(2)}) %collective-permute-start.19) | collective-permute-done | bytes 131104 | tf_op jit(solution)/shard_map/ppermute | solution.py:43
  147.2 4.8 %collective-permute-start.21 = (bf16[32,512]{1,0:T(8,128)(2,1)S(1)}, bf16[32,512]{1,0:T(8,128)(2,1)S(1)}, u32[]{:S(2)}, u32[]{:S(2)}) collective-permute-start(bf16[32,512]{1,0:T(8,128)(2,1)S(1)} %get-tuple-element.85), channel_id=1, source_target_pairs={{0,6},{1,7},{2,0},{3,1},{4,2},{5,3},{6,4},{7,5},{8,14},{9,15},{10,... | collective-permute-start | bytes 98312 | tf_op jit(solution)/shard_map/ppermute | solution.py:39
  153.5 4.0 %collective-permute-done.22.a2 = bf16[32,512]{1,0:T(8,128)(2,1)S(1)} collective-permute-done((bf16[32,512]{1,0:T(8,128)(2,1)S(1)}, bf16[32,512]{1,0:T(8,128)(2,1)S(1)}, u32[]{:S(2)}, u32[]{:S(2)}) %collective-permute-start.22) | collective-permute-done | bytes 32800 | tf_op jit(solution)/shard_map/ppermute | solution.py:39
  164.5 3.4 %collective-permute-start.27 = (bf16[128,512]{1,0:T(8,128)(2,1)S(1)}, bf16[128,512]{1,0:T(8,128)(2,1)S(1)}, u32[]{:S(2)}, u32[]{:S(2)}) collective-permute-start(bf16[128,512]{1,0:T(8,128)(2,1)S(1)} %shard_map.140.rank), channel_id=1, source_target_pairs={{0,1},{1,0},{2,3},{3,2},{4,5},{5,4},{6,7},{7,6},{8,9},{9,8},{10,11... | collective-permute-start | bytes 393224 | tf_op jit(solution)/shard_map/ppermute | solution.py:35
  169.6 3.8 %collective-permute-start.16 = (bf16[256,256]{1,0:T(8,128)(2,1)S(1)}, bf16[256,256]{1,0:T(8,128)(2,1)S(1)}, u32[]{:S(2)}, u32[]{:S(2)}) collective-permute-start(bf16[256,256]{1,0:T(8,128)(2,1)S(1)} %get-tuple-element.90), channel_id=1, source_target_pairs={{0,16},{1,17},{2,18},{3,19},{4,20},{5,21},{6,22},{7,23},{8,24},{9,... | collective-permute-start | bytes 393224 | tf_op jit(solution)/shard_map/ppermute | solution.py:43
  173.7 5.5 %collective-permute-done.17.a3 = bf16[256,256]{1,0:T(8,128)(2,1)S(1)} collective-permute-done((bf16[256,256]{1,0:T(8,128)(2,1)S(1)}, bf16[256,256]{1,0:T(8,128)(2,1)S(1)}, u32[]{:S(2)}, u32[]{:S(2)}) %collective-permute-start.17) | collective-permute-done | bytes 131104 | tf_op jit(solution)/shard_map/ppermute | solution.py:43
  179.2 4.8 %collective-permute-done.16.a2 = bf16[256,256]{1,0:T(8,128)(2,1)S(1)} collective-permute-done((bf16[256,256]{1,0:T(8,128)(2,1)S(1)}, bf16[256,256]{1,0:T(8,128)(2,1)S(1)}, u32[]{:S(2)}, u32[]{:S(2)}) %collective-permute-start.16) | collective-permute-done | bytes 131104 | tf_op jit(solution)/shard_map/ppermute | solution.py:43
  184.0 3.3 %collective-permute-done.15.a1 = bf16[256,256]{1,0:T(8,128)(2,1)S(1)} collective-permute-done((bf16[256,256]{1,0:T(8,128)(2,1)S(1)}, bf16[256,256]{1,0:T(8,128)(2,1)S(1)}, u32[]{:S(2)}, u32[]{:S(2)}) %collective-permute-start.15) | collective-permute-done | bytes 131104 | tf_op jit(solution)/shard_map/ppermute | solution.py:43
  (105 shorter events, 56.6 us)
Async XLA Ops:
  9.6 27.3 %all-to-all-start = ((bf16[8,64,1792]{2,1,0:T(8,128)(2,1)}), bf16[8,64,1792]{2,1,0:T(8,128)(2,1)S(1)}, u32[]{:S(2)}, u32[]{:S(2)}) async-start(bf16[8,64,1792]{2,1,0:T(8,128)(2,1)} %broadcast_in_dim.11), calls=%async_computation | async-start | bytes 3670016 | tf_op jit(solution)/shard_map/all_to_all | solution.py:51
  15.1 89.4 %all-gather.3.cloned.1.call-start = ((), (), s32[]{:S(2)}) async-start(), calls=%async_computation.5 | async-start | bytes 4325376 | tf_op jit(solution)/shard_map/all_gather | solution.py:413
  36.9 40.5 %collective-permute-start.7 = (bf16[8,64,1792]{2,1,0:T(8,128)(2,1)S(1)}, bf16[8,64,1792]{2,1,0:T(8,128)(2,1)}, u32[]{:S(2)}, u32[]{:S(2)}) collective-permute-start(bf16[8,64,1792]{2,1,0:T(8,128)(2,1)S(1)} %all-to-all-done.refs_2_.early), channel_id=1, source_target_pairs={{0,1},{1,0},{2,3},{3,2},{4,5},{5,4},{6,7},{7,6},{8,9},{9,8},{10,11... | collective-permute-start | bytes 5505032 | tf_op jit(solution)/shard_map/ppermute | solution.py:35
  41.6 9.4 %collective-permute-start.4 = (bf16[128,1024]{1,0:T(8,128)(2,1)}, bf16[128,1024]{1,0:T(8,128)(2,1)S(1)}, u32[]{:S(2)}, u32[]{:S(2)}) collective-permute-start(bf16[128,1024]{1,0:T(8,128)(2,1)} %copy-done.19), channel_id=1, source_target_pairs={{0,6},{1,7},{2,0},{3,1},{4,2},{5,3},{6,4},{7,5},{8,14},{9,15},{10,... | collective-permute-start | bytes 786440 | tf_op jit(solution)/shard_map/ppermute | solution.py:39
  44.2 9.5 %collective-permute-start.5 = (bf16[128,1024]{1,0:T(8,128)(2,1)}, bf16[128,1024]{1,0:T(8,128)(2,1)S(1)}, u32[]{:S(2)}, u32[]{:S(2)}) collective-permute-start(bf16[128,1024]{1,0:T(8,128)(2,1)} %copy-done.18), channel_id=1, source_target_pairs={{0,4},{1,5},{2,6},{3,7},{4,0},{5,1},{6,2},{7,3},{8,12},{9,13},{10,... | collective-permute-start | bytes 786440 | tf_op jit(solution)/shard_map/ppermute | solution.py:39
  44.7 15.3 %collective-permute-start.6 = (bf16[128,1024]{1,0:T(8,128)(2,1)}, bf16[128,1024]{1,0:T(8,128)(2,1)S(1)}, u32[]{:S(2)}, u32[]{:S(2)}) collective-permute-start(bf16[128,1024]{1,0:T(8,128)(2,1)} %copy-done.17), channel_id=1, source_target_pairs={{0,2},{1,3},{2,4},{3,5},{4,6},{5,7},{6,0},{7,1},{8,10},{9,11},{10,... | collective-permute-start | bytes 786440 | tf_op jit(solution)/shard_map/ppermute | solution.py:39
  60.0 35.9 %all-to-all-start.1 = ((bf16[16,8,1536]{2,1,0:T(8,128)(2,1)}), bf16[16,8,1536]{2,1,0:T(8,128)(2,1)S(1)}, u32[]{:S(2)}, u32[]{:S(2)}) async-start(bf16[16,8,1536]{2,1,0:T(8,128)(2,1)} %shard_map.129), calls=%async_computation.1 | async-start | bytes 786432 | tf_op jit(solution)/shard_map/all_to_all | solution.py:51
  69.7 13.6 %collective-permute-start.8 = (bf16[128,256]{1,0:T(8,128)(2,1)S(1)}, bf16[128,256]{1,0:T(8,128)(2,1)S(1)}, u32[]{:S(2)}, u32[]{:S(2)}) collective-permute-start(bf16[128,256]{1,0:T(8,128)(2,1)S(1)} %get-tuple-element.65), channel_id=1, source_target_pairs={{0,24},{1,25},{2,26},{3,27},{4,28},{5,29},{6,30},{7,31},{8,0},{9,1... | collective-permute-start | bytes 196616 | tf_op jit(solution)/shard_map/ppermute | solution.py:43
  73.2 21.5 %collective-permute-start.9 = (bf16[128,256]{1,0:T(8,128)(2,1)S(1)}, bf16[128,256]{1,0:T(8,128)(2,1)S(1)}, u32[]{:S(2)}, u32[]{:S(2)}) collective-permute-start(bf16[128,256]{1,0:T(8,128)(2,1)S(1)} %get-tuple-element.66), channel_id=1, source_target_pairs={{0,16},{1,17},{2,18},{3,19},{4,20},{5,21},{6,22},{7,23},{8,24},{9,... | collective-permute-start | bytes 196616 | tf_op jit(solution)/shard_map/ppermute | solution.py:43
  75.3 20.0 %collective-permute-start.10 = (bf16[128,256]{1,0:T(8,128)(2,1)S(1)}, bf16[128,256]{1,0:T(8,128)(2,1)S(1)}, u32[]{:S(2)}, u32[]{:S(2)}) collective-permute-start(bf16[128,256]{1,0:T(8,128)(2,1)S(1)} %get-tuple-element.67), channel_id=1, source_target_pairs={{0,8},{1,9},{2,10},{3,11},{4,12},{5,13},{6,14},{7,15},{8,16},{9,17... | collective-permute-start | bytes 196616 | tf_op jit(solution)/shard_map/ppermute | solution.py:43
  95.9 20.8 %collective-permute-start.11 = (bf16[256,8192]{1,0:T(8,128)(2,1)}, bf16[256,8192]{1,0:T(8,128)(2,1)}, u32[]{:S(2)}, u32[]{:S(2)}) collective-permute-start(bf16[256,8192]{1,0:T(8,128)(2,1)} %w.1), channel_id=1, source_target_pairs={{0,1},{1,0},{2,3},{3,2},{4,5},{5,4},{6,7},{7,6},{8,9},{9,8},{10,11... | collective-permute-start | bytes 12582920 | tf_op jit(solution)/shard_map/ppermute | solution.py:35
  98.1 18.6 %all-to-all-start.2 = ((bf16[16,8,1536]{2,1,0:T(8,128)(2,1)}), bf16[16,8,1536]{2,1,0:T(8,128)(2,1)S(1)}, u32[]{:S(2)}, u32[]{:S(2)}) async-start(bf16[16,8,1536]{2,1,0:T(8,128)(2,1)} %shard_map.132), calls=%async_computation.2 | async-start | bytes 786432 | tf_op jit(solution)/shard_map/all_to_all | solution.py:51
  104.5 63.5 %reduce-scatter.2.cloned.1.call-start = ((), (), s32[]{:S(2)}) async-start(), calls=%async_computation.4 | async-start | bytes 2621440 | tf_op jit(solution)/shard_map/reduce_scatter | solution.py:475
  111.3 5.4 %collective-permute-start.12 = (f32[128,256]{1,0:T(8,128)S(1)}, f32[128,256]{1,0:T(8,128)S(1)}, u32[]{:S(2)}, u32[]{:S(2)}) collective-permute-start(f32[128,256]{1,0:T(8,128)S(1)} %get-tuple-element.70), channel_id=1, source_target_pairs={{0,1},{1,0},{2,3},{3,2},{4,5},{5,4},{6,7},{7,6},{8,9},{9,8},{10,11... | collective-permute-start | bytes 393224 | tf_op jit(solution)/shard_map/ppermute | solution.py:35
  129.8 7.4 %collective-permute-start.20 = (bf16[128,512]{1,0:T(8,128)(2,1)S(1)}, bf16[128,512]{1,0:T(8,128)(2,1)S(1)}, u32[]{:S(2)}, u32[]{:S(2)}) collective-permute-start(bf16[128,512]{1,0:T(8,128)(2,1)S(1)} %shard_map.136.a0), channel_id=1, source_target_pairs={{0,8},{1,9},{2,10},{3,11},{4,12},{5,13},{6,14},{7,15},{8,16},{9,17... | collective-permute-start | bytes 393224 | tf_op jit(solution)/shard_map/ppermute | solution.py:43
  129.9 15.4 %collective-permute-start.19 = (bf16[128,512]{1,0:T(8,128)(2,1)S(1)}, bf16[128,512]{1,0:T(8,128)(2,1)S(1)}, u32[]{:S(2)}, u32[]{:S(2)}) collective-permute-start(bf16[128,512]{1,0:T(8,128)(2,1)S(1)} %shard_map.136.a0), channel_id=1, source_target_pairs={{0,16},{1,17},{2,18},{3,19},{4,20},{5,21},{6,22},{7,23},{8,24},{9,... | collective-permute-start | bytes 393224 | tf_op jit(solution)/shard_map/ppermute | solution.py:43
  135.6 10.9 %collective-permute-start.18 = (bf16[128,512]{1,0:T(8,128)(2,1)S(1)}, bf16[128,512]{1,0:T(8,128)(2,1)S(1)}, u32[]{:S(2)}, u32[]{:S(2)}) collective-permute-start(bf16[128,512]{1,0:T(8,128)(2,1)S(1)} %shard_map.136.a0), channel_id=1, source_target_pairs={{0,24},{1,25},{2,26},{3,27},{4,28},{5,29},{6,30},{7,31},{8,0},{9,1... | collective-permute-start | bytes 393224 | tf_op jit(solution)/shard_map/ppermute | solution.py:43
  147.2 6.3 %collective-permute-start.21 = (bf16[32,512]{1,0:T(8,128)(2,1)S(1)}, bf16[32,512]{1,0:T(8,128)(2,1)S(1)}, u32[]{:S(2)}, u32[]{:S(2)}) collective-permute-start(bf16[32,512]{1,0:T(8,128)(2,1)S(1)} %get-tuple-element.85), channel_id=1, source_target_pairs={{0,6},{1,7},{2,0},{3,1},{4,2},{5,3},{6,4},{7,5},{8,14},{9,15},{10,... | collective-permute-start | bytes 98312 | tf_op jit(solution)/shard_map/ppermute | solution.py:39
  152.0 5.5 %collective-permute-start.22 = (bf16[32,512]{1,0:T(8,128)(2,1)S(1)}, bf16[32,512]{1,0:T(8,128)(2,1)S(1)}, u32[]{:S(2)}, u32[]{:S(2)}) collective-permute-start(bf16[32,512]{1,0:T(8,128)(2,1)S(1)} %get-tuple-element.86), channel_id=1, source_target_pairs={{0,4},{1,5},{2,6},{3,7},{4,0},{5,1},{6,2},{7,3},{8,12},{9,13},{10,... | collective-permute-start | bytes 98312 | tf_op jit(solution)/shard_map/ppermute | solution.py:39
  152.6 5.8 %collective-permute-start.23 = (bf16[32,512]{1,0:T(8,128)(2,1)S(1)}, bf16[32,512]{1,0:T(8,128)(2,1)S(1)}, u32[]{:S(2)}, u32[]{:S(2)}) collective-permute-start(bf16[32,512]{1,0:T(8,128)(2,1)S(1)} %get-tuple-element.87), channel_id=1, source_target_pairs={{0,2},{1,3},{2,4},{3,5},{4,6},{5,7},{6,0},{7,1},{8,10},{9,11},{10,... | collective-permute-start | bytes 98312 | tf_op jit(solution)/shard_map/ppermute | solution.py:39
  164.5 9.2 %collective-permute-start.27 = (bf16[128,512]{1,0:T(8,128)(2,1)S(1)}, bf16[128,512]{1,0:T(8,128)(2,1)S(1)}, u32[]{:S(2)}, u32[]{:S(2)}) collective-permute-start(bf16[128,512]{1,0:T(8,128)(2,1)S(1)} %shard_map.140.rank), channel_id=1, source_target_pairs={{0,1},{1,0},{2,3},{3,2},{4,5},{5,4},{6,7},{7,6},{8,9},{9,8},{10,11... | collective-permute-start | bytes 393224 | tf_op jit(solution)/shard_map/ppermute | solution.py:35
  169.0 10.1 %collective-permute-start.17 = (bf16[256,256]{1,0:T(8,128)(2,1)S(1)}, bf16[256,256]{1,0:T(8,128)(2,1)S(1)}, u32[]{:S(2)}, u32[]{:S(2)}) collective-permute-start(bf16[256,256]{1,0:T(8,128)(2,1)S(1)} %get-tuple-element.89), channel_id=1, source_target_pairs={{0,8},{1,9},{2,10},{3,11},{4,12},{5,13},{6,14},{7,15},{8,16},{9,17... | collective-permute-start | bytes 393224 | tf_op jit(solution)/shard_map/ppermute | solution.py:43
  169.6 14.4 %collective-permute-start.16 = (bf16[256,256]{1,0:T(8,128)(2,1)S(1)}, bf16[256,256]{1,0:T(8,128)(2,1)S(1)}, u32[]{:S(2)}, u32[]{:S(2)}) collective-permute-start(bf16[256,256]{1,0:T(8,128)(2,1)S(1)} %get-tuple-element.90), channel_id=1, source_target_pairs={{0,16},{1,17},{2,18},{3,19},{4,20},{5,21},{6,22},{7,23},{8,24},{9,... | collective-permute-start | bytes 393224 | tf_op jit(solution)/shard_map/ppermute | solution.py:43
  173.4 14.0 %collective-permute-start.15 = (bf16[256,256]{1,0:T(8,128)(2,1)S(1)}, bf16[256,256]{1,0:T(8,128)(2,1)S(1)}, u32[]{:S(2)}, u32[]{:S(2)}) collective-permute-start(bf16[256,256]{1,0:T(8,128)(2,1)S(1)} %get-tuple-element.91), channel_id=1, source_target_pairs={{0,24},{1,25},{2,26},{3,27},{4,28},{5,29},{6,30},{7,31},{8,0},{9,1... | collective-permute-start | bytes 393224 | tf_op jit(solution)/shard_map/ppermute | solution.py:43
  (29 other events, 140.6 us)
Sparse Core Ops, SparseCore 0:
  18.5 73.1 all-gather.2
  129.9 31.3 reduce-scatter.1
